TPU v7x, 512 devices: a whole 4x8x8 slice. The times are simulated.
512 devices in a mesh: dp: 16 (over x, z_hi), ctx: 32 (over y, z_lo, core).
Axes of the slice: x: 4, y: 8, z: 8 (z_hi: 4, z_lo: 2; z = z_hi * 2 + z_lo), core: 2. Of those that a mesh axis runs over, the one named last changes fastest.
Arguments:
- u_saved: bfloat16 [16, 4096, 2048], P('dp', 'ctx'), may hold values from -6 to 6
- grad_out: bfloat16 [16, 4096, 2048], P('dp', 'ctx'), may hold values from -6 to 6
- filters: bfloat16 [4096, 128], P('ctx'), may hold values from -2 to 2
Outputs:
- input_grad: bfloat16 [16, 4096, 2048], P('dp', 'ctx')
- filter_grad: float32 [4096, 128], P('ctx', 'dp')
All inputs are finite; a program needn't handle non-finite values.
Results may differ from a plain program's by a relative error of at most 0.001.
Values may be sent and summed in bfloat16 or wider, within the bound.
No kernel may reach another device: no remote copies, remote signals or barrier semaphores. Data moves between devices by JAX's collectives and lax.ppermute only.
A program may use at most 128 MiB of HBM per device.

v0:
```python
import functools

import jax
import jax.numpy as jnp
from jax import lax
from jax.experimental import pallas as pl
from jax.experimental.pallas import tpu as pltpu
from jax.sharding import PartitionSpec as P

GROUP = 16
LANES = 128
VMEM_LIMIT = 56 * 1024 * 1024


def widen_blocks(blocks_ref, group, wide_ref):
    parts = blocks_ref.shape[0]
    first = pl.multiple_of(group * GROUP, GROUP)
    for part in range(parts):
        row = (part // 2) * GROUP
        lane = (part % 2) * LANES
        wide_ref[row : row + GROUP, lane : lane + LANES] = blocks_ref[
            part, pl.ds(first, GROUP), :
        ]


def input_kernel(grad_ref, filt_ref, out_ref, wide_ref, toep_ref):
    parts, channels, _ = grad_ref.shape
    half = parts // 2
    rows = half * GROUP
    span = 2 * LANES
    wide_ref[rows:, :] = jnp.zeros_like(wide_ref[rows:, :])

    def per_group(group, carry):
        widen_blocks(grad_ref, group, wide_ref)
        line = filt_ref[pl.ds(group, 1), :]
        spread = jnp.broadcast_to(line, (LANES, line.shape[1]))
        toep_ref[...] = pltpu.roll(spread, 0, 1, stride=1, stride_axis=0).astype(jnp.bfloat16)
        total = jnp.zeros((rows, span), jnp.float32)
        for lag in range(half):
            start = lag * span
            taps = jnp.concatenate(
                [
                    toep_ref[:, start + LANES : start + LANES + span],
                    toep_ref[:, start : start + span],
                ],
                axis=0,
            )
            total = total + lax.dot_general(
                wide_ref[lag * GROUP : lag * GROUP + rows, :],
                taps,
                (((1,), (1,)), ((), ())),
                preferred_element_type=jnp.float32,
            )
        done = total.astype(jnp.bfloat16)
        first = pl.multiple_of(group * GROUP, GROUP)
        for part in range(parts):
            row = (part // 2) * GROUP
            lane = (part % 2) * LANES
            out_ref[part, pl.ds(first, GROUP), :] = done[
                row : row + GROUP, lane : lane + LANES
            ]
        return carry

    lax.fori_loop(0, channels // GROUP, per_group, 0)


def filter_kernel(grad_ref, saved_ref, out_ref, wide_ref, saved_wide_ref, toep_ref):
    parts, channels, _ = grad_ref.shape
    half = parts // 2
    rows = half * GROUP
    span = 2 * LANES
    length = parts * LANES
    wide_ref[rows:, :] = jnp.zeros_like(wide_ref[rows:, :])
    row_ids = lax.broadcasted_iota(jnp.int32, (span, span), 0)
    col_ids = lax.broadcasted_iota(jnp.int32, (span, span), 1)
    mirror = (row_ids // LANES) * LANES + (LANES - 1 - row_ids % LANES)
    flip = jnp.where(mirror == col_ids, 1.0, 0.0).astype(jnp.bfloat16)

    def per_group(group, carry):
        widen_blocks(grad_ref, group, wide_ref)
        widen_blocks(saved_ref, group, saved_wide_ref)
        saved_lag = lax.dot_general(
            flip,
            saved_wide_ref[...],
            (((1,), (1,)), ((), ())),
            preferred_element_type=jnp.float32,
        ).astype(jnp.bfloat16)
        toep_ref[...] = jnp.zeros_like(toep_ref)
        for lag in range(half):
            start = lag * span
            piece = jnp.dot(
                saved_lag,
                wide_ref[lag * GROUP : lag * GROUP + rows, :],
                preferred_element_type=jnp.float32,
            )
            toep_ref[:, start + LANES : start + LANES + span] += piece[:LANES, :]
            toep_ref[:, start : start + span] += piece[LANES:, :]
        turned = pltpu.roll(toep_ref[...], 1, 1, stride=1, stride_axis=0)
        out_ref[pl.ds(group, 1), :] = jnp.sum(turned, axis=0, keepdims=True)[
            :, span : span + length
        ]
        return carry

    lax.fori_loop(0, channels // GROUP, per_group, 0)


def input_pass(grad_blocks, filter_line):
    parts, channels, _ = grad_blocks.shape
    rows = parts // 2 * GROUP
    return pl.pallas_call(
        input_kernel,
        out_shape=jax.ShapeDtypeStruct(grad_blocks.shape, jnp.bfloat16),
        scratch_shapes=[
            pltpu.VMEM((2 * rows, 2 * LANES), jnp.bfloat16),
            pltpu.VMEM((LANES, filter_line.shape[1]), jnp.bfloat16),
        ],
        compiler_params=pltpu.CompilerParams(vmem_limit_bytes=VMEM_LIMIT),
        cost_estimate=pl.CostEstimate(flops=2**31, bytes_accessed=2**20, transcendentals=0),
    )(grad_blocks, filter_line)


def filter_pass(grad_blocks, saved_blocks):
    parts, channels, _ = grad_blocks.shape
    rows = parts // 2 * GROUP
    length = parts * LANES
    return pl.pallas_call(
        filter_kernel,
        out_shape=jax.ShapeDtypeStruct((channels // GROUP, length), jnp.float32),
        scratch_shapes=[
            pltpu.VMEM((2 * rows, 2 * LANES), jnp.bfloat16),
            pltpu.VMEM((rows, 2 * LANES), jnp.bfloat16),
            pltpu.VMEM((LANES, length + 2 * LANES), jnp.float32),
        ],
        compiler_params=pltpu.CompilerParams(vmem_limit_bytes=VMEM_LIMIT),
        cost_estimate=pl.CostEstimate(flops=2**31, bytes_accessed=2**20, transcendentals=0),
    )(grad_blocks, saved_blocks)


def to_channels(tokens_by_channel, parts):
    turned = tokens_by_channel.T
    blocks = turned.reshape(parts, turned.shape[0] // parts, turned.shape[1])
    return lax.all_to_all(blocks, "ctx", split_axis=0, concat_axis=0, tiled=True)


def on_device(u_saved, grad_out, filters):
    parts = lax.axis_size("ctx")
    seqs = lax.axis_size("dp")
    filter_blocks = to_channels(filters, parts)
    grad_blocks = to_channels(grad_out[0], parts)
    saved_blocks = to_channels(u_saved[0], parts)
    groups_here = filter_blocks.shape[1]
    length = parts * filter_blocks.shape[2]
    line = filter_blocks.transpose(1, 0, 2).reshape(groups_here, length).astype(jnp.float32)
    line = jnp.pad(line, ((0, 0), (LANES, LANES)))
    input_blocks = input_pass(grad_blocks, line)
    returned = lax.all_to_all(input_blocks, "ctx", split_axis=0, concat_axis=0, tiled=True)
    input_grad = returned.reshape(-1, returned.shape[2]).T[None]
    group_lags = filter_pass(grad_blocks, saved_blocks)
    lag_blocks = group_lags.reshape(groups_here, parts, -1).transpose(1, 0, 2)
    lag_moved = lax.all_to_all(lag_blocks, "ctx", split_axis=0, concat_axis=0, tiled=True)
    by_group = lag_moved.reshape(-1, lag_moved.shape[2])
    filter_part = lax.psum_scatter(by_group, "dp", scatter_dimension=0, tiled=True)
    filter_grad = filter_part.T / jnp.sqrt(jnp.float32(GROUP * seqs * length))
    return (input_grad, filter_grad)


def solution(mesh):
    in_specs = (P("dp", "ctx", None), P("dp", "ctx", None), P("ctx", None))
    out_specs = (P("dp", "ctx", None), P("ctx", "dp"))
    return jax.shard_map(
        on_device, mesh=mesh, in_specs=in_specs, out_specs=out_specs, check_vma=False
    )
```

profile of v0, /device:TPU:8, one launch (start us, length us, event | category | flops | bytes accessed | tf_op | source)
XLA Modules:
  0.0 273.1 jit_solution(14524473410712276945)
XLA Ops:
  7.2 1.5 copy.16
  8.6 9.5 %all-to-all-start.1 = ((bf16[32,4,128]{2,1,0:T(4,128)(2,1)}), bf16[32,4,128]{2,1,0:T(4,128)(2,1)S(1)}, u32[]{:S(2)}, u32[]{:S(2)}) async-start(bf16[32,4,128]{2,1,0:T(4,128)(2,1)} %bitcast.4), calls=%async_computation.1 | async-start | bytes 65536 | tf_op jit(solution)/shard_map/all_to_all | solution.py:142
  18.2 2.0 copy.18
  20.2 5.2 %all-to-all-done.1 = bf16[32,4,128]{2,1,0:T(4,128)(2,1)S(1)} async-done(((bf16[32,4,128]{2,1,0:T(4,128)(2,1)}), bf16[32,4,128]{2,1,0:T(4,128)(2,1)S(1)}, u32[]{:S(2)}, u32[]{:S(2)}) %all-to-all-start.1) | async-done | bytes 32800 | tf_op jit(solution)/shard_map/all_to_all | solution.py:142
  25.4 5.0 %all-to-all-start.3 = ((bf16[32,64,128]{2,1,0:T(8,128)(2,1)}), bf16[32,64,128]{2,1,0:T(8,128)(2,1)S(1)}, u32[]{:S(2)}, u32[]{:S(2)}) async-start(bf16[32,64,128]{2,1,0:T(8,128)(2,1)} %bitcast.12), calls=%async_computation.3 | async-start | bytes 1048576 | tf_op jit(solution)/shard_map/all_to_all | solution.py:142
  30.4 1.0 copy.15
  31.4 15.9 %all-to-all-done.3.saved_ref = bf16[32,64,128]{2,1,0:T(8,128)(2,1)S(1)} async-done(((bf16[32,64,128]{2,1,0:T(8,128)(2,1)}), bf16[32,64,128]{2,1,0:T(8,128)(2,1)S(1)}, u32[]{:S(2)}, u32[]{:S(2)}) %all-to-all-start.3) | async-done | bytes 524320 | tf_op jit(solution)/shard_map/all_to_all | solution.py:142
  47.3 0.8 copy-done.1
  48.1 5.0 %all-to-all-start = ((bf16[32,64,128]{2,1,0:T(8,128)(2,1)}), bf16[32,64,128]{2,1,0:T(8,128)(2,1)S(1)}, u32[]{:S(2)}, u32[]{:S(2)}) async-start(bf16[32,64,128]{2,1,0:T(8,128)(2,1)} %bitcast.2), calls=%async_computation | async-start | bytes 1048576 | tf_op jit(solution)/shard_map/all_to_all | solution.py:142
  53.1 0.6 pad_convert_fusion.filt_ref
  53.7 16.3 %all-to-all-done.grad_ref = bf16[32,64,128]{2,1,0:T(8,128)(2,1)S(1)} async-done(((bf16[32,64,128]{2,1,0:T(8,128)(2,1)}), bf16[32,64,128]{2,1,0:T(8,128)(2,1)S(1)}, u32[]{:S(2)}, u32[]{:S(2)}) %all-to-all-start) | async-done | bytes 524320 | tf_op jit(solution)/shard_map/all_to_all | solution.py:142
  70.0 0.8 copy-done.2
  70.8 6.1 %shard_map.51 = f32[4,4096]{1,0:T(4,128)} custom-call(bf16[32,64,128]{2,1,0:T(8,128)(2,1)} %copy-done.2, bf16[32,64,128]{2,1,0:T(8,128)(2,1)} %copy-done.1), custom_call_target="tpu_custom_call" | custom-call | flops 2147483648 | bytes 1048576 | tf_op jit(solution)/shard_map/pallas_call | solution.py:126
  76.9 4.9 %all-to-all-start.4 = ((f32[32,4,128]{2,1,0:T(4,128)}), f32[32,4,128]{2,1,0:T(4,128)S(1)}, u32[]{:S(2)}, u32[]{:S(2)}) async-start(f32[32,4,128]{2,1,0:T(4,128)} %bitcast.31), calls=%async_computation.4 | async-start | bytes 131072 | tf_op jit(solution)/shard_map/all_to_all | solution.py:160
  81.8 5.4 %shard_map.50 = bf16[32,64,128]{2,1,0:T(8,128)(2,1)} custom-call(bf16[32,64,128]{2,1,0:T(8,128)(2,1)} %copy-done.2, f32[4,4352]{1,0:T(4,128)} %pad_convert_fusion.filt_ref), custom_call_target="tpu_custom_call" | custom-call | flops 2147483648 | bytes 1048576 | tf_op jit(solution)/shard_map/pallas_call | solution.py:110
  87.3 2.3 all-to-all-done.4
  89.5 0.6 copy-done.3
  90.2 6.1 %all-to-all-start.2 = ((bf16[32,64,128]{2,1,0:T(8,128)(2,1)}), bf16[32,64,128]{2,1,0:T(8,128)(2,1)S(1)}, u32[]{:S(2)}, u32[]{:S(2)}) async-start(bf16[32,64,128]{2,1,0:T(8,128)(2,1)} %shard_map.50), calls=%async_computation.2 | async-start | bytes 1048576 | tf_op jit(solution)/shard_map/all_to_all | solution.py:156
  96.3 0.0 all-reduce.4.cloned.1.call-start
  96.3 0.7 all-reduce.4.cloned.1.call-update
  97.0 1.3 dynamic-slice
  98.9 165.1 %all-reduce.4.cloned.1.call-done = f32[128,128]{1,0:T(8,128)} async-done(((f32[128,128]{1,0:T(8,128)}), f32[128,128]{1,0:T(8,128)}) %all-reduce.4.cloned.1.call-update) | async-done | bytes 65552
  264.0 1.3 fusion
  265.3 1.0 copy.17
  (6 shorter events, 0.0 us)
Async XLA Ops:
  8.6 16.8 %all-to-all-start.1 = ((bf16[32,4,128]{2,1,0:T(4,128)(2,1)}), bf16[32,4,128]{2,1,0:T(4,128)(2,1)S(1)}, u32[]{:S(2)}, u32[]{:S(2)}) async-start(bf16[32,4,128]{2,1,0:T(4,128)(2,1)} %bitcast.4), calls=%async_computation.1 | async-start | bytes 65536 | tf_op jit(solution)/shard_map/all_to_all | solution.py:142
  25.4 5.0 %copy-start = (bf16[1,128,2048]{2,1,0:T(8,128)(2,1)S(1)}, bf16[1,128,2048]{2,1,0:T(8,128)(2,1)}, u32[]{:S(2)}) copy-start(bf16[1,128,2048]{2,1,0:T(8,128)(2,1)} %param.4) | copy-start | bytes 1572868
  25.4 21.9 %all-to-all-start.3 = ((bf16[32,64,128]{2,1,0:T(8,128)(2,1)}), bf16[32,64,128]{2,1,0:T(8,128)(2,1)S(1)}, u32[]{:S(2)}, u32[]{:S(2)}) async-start(bf16[32,64,128]{2,1,0:T(8,128)(2,1)} %bitcast.12), calls=%async_computation.3 | async-start | bytes 1048576 | tf_op jit(solution)/shard_map/all_to_all | solution.py:142
  47.3 0.8 copy-start.1
  48.1 21.9 %all-to-all-start = ((bf16[32,64,128]{2,1,0:T(8,128)(2,1)}), bf16[32,64,128]{2,1,0:T(8,128)(2,1)S(1)}, u32[]{:S(2)}, u32[]{:S(2)}) async-start(bf16[32,64,128]{2,1,0:T(8,128)(2,1)} %bitcast.2), calls=%async_computation | async-start | bytes 1048576 | tf_op jit(solution)/shard_map/all_to_all | solution.py:142
  70.0 0.8 copy-start.2
  76.9 12.7 %all-to-all-start.4 = ((f32[32,4,128]{2,1,0:T(4,128)}), f32[32,4,128]{2,1,0:T(4,128)S(1)}, u32[]{:S(2)}, u32[]{:S(2)}) async-start(f32[32,4,128]{2,1,0:T(4,128)} %bitcast.31), calls=%async_computation.4 | async-start | bytes 131072 | tf_op jit(solution)/shard_map/all_to_all | solution.py:160
  89.5 0.6 copy-start.3
  90.2 175.1 %all-to-all-start.2 = ((bf16[32,64,128]{2,1,0:T(8,128)(2,1)}), bf16[32,64,128]{2,1,0:T(8,128)(2,1)S(1)}, u32[]{:S(2)}, u32[]{:S(2)}) async-start(bf16[32,64,128]{2,1,0:T(8,128)(2,1)} %shard_map.50), calls=%async_computation.2 | async-start | bytes 1048576 | tf_op jit(solution)/shard_map/all_to_all | solution.py:156
  96.3 167.8 %all-reduce.4.cloned.1.call-start = ((), (), s32[]{:S(2)}) async-start(), calls=%async_computation.5 | async-start | bytes 131072
Sparse Core Ops, SparseCore 0:
  100.6 163.3 all-reduce.3
where the time goes:
time: 274 us; the launch traced here: 273 us
  waiting for transfers between devices  205 us (75%)
  starting transfers between devices  30.6 us (11%)
  between operations  14.7 us (5%)
  Pallas kernels  11.5 us (4%)
  local copies, waits for them, and re-layouts  9.01 us (3%)
    unnamed x2, waiting for transfers between devices  166 us
    all_to_all x3, waiting for transfers between devices, to_channels(): lax.all_to_all(blocks, 'ctx', split_axis=0, concat_axis=0, tiled=True)  37.4 us
    all_to_all x3, starting transfers between devices, to_channels(): lax.all_to_all(blocks, 'ctx', split_axis=0, concat_axis=0, tiled=True)  19.5 us
    all_to_all x1, starting transfers between devices, on_device(): lax.all_to_all(input_blocks, 'ctx', split_axis=0, concat_axis=0, tiled=True)  6.1 us
    pallas_call x1, Pallas kernels, filter_pass(): pl.pallas_call(filter_kernel, out_shape=jax.ShapeDtypeStruct((channels //...  6.06 us
  transfers between devices with their start and end apart: 6, of which 5 were waited for; matrix products, arithmetic and copies ran while one was open for 2% of the time, Pallas kernels for 2%

commit v1 on v0

v1 whole, which is shorter than its diff:
```python
import math

import jax
import jax.numpy as jnp
from jax import lax
from jax.experimental import pallas as pl
from jax.experimental.pallas import tpu as pltpu
from jax.sharding import PartitionSpec as P

GROUP = 16
LANES = 128
SPAN = 2 * LANES
SIDE = 4
MIB = 1024 * 1024


def call(kernel, out_shape, *operands, scratch=(), flops=2**20, vmem=2 * MIB):
    in_vmem = pl.BlockSpec(memory_space=pltpu.VMEM)
    several = isinstance(out_shape, (list, tuple))
    return pl.pallas_call(
        kernel,
        out_shape=out_shape,
        in_specs=[in_vmem] * len(operands),
        out_specs=[in_vmem] * len(out_shape) if several else in_vmem,
        scratch_shapes=list(scratch),
        compiler_params=pltpu.CompilerParams(vmem_limit_bytes=vmem),
        cost_estimate=pl.CostEstimate(flops=flops, bytes_accessed=2**20, transcendentals=0),
    )(*operands)


def pack_kernel(saved_ref, grad_ref, filt_ref, out_ref):
    parts, rows, _ = out_ref.shape
    channels = saved_ref.shape[1] // parts
    groups = filt_ref.shape[1] // parts
    per_tile = LANES // channels
    for tile in range(parts // per_tile):
        cols = slice(tile * LANES, (tile + 1) * LANES)
        grad_rows = grad_ref[:, cols].T
        saved_rows = saved_ref[:, cols].T
        for inner in range(per_tile):
            part = tile * per_tile + inner
            mine = slice(inner * channels, (inner + 1) * channels)
            out_ref[part, :channels, :] = grad_rows[mine, :]
            out_ref[part, channels : 2 * channels, :] = saved_rows[mine, :]
    lines = filt_ref[...].astype(jnp.float32).T
    tail = rows - 2 * channels
    for part in range(parts):
        mine = lines[part * groups : (part + 1) * groups, :]
        block = jnp.concatenate([mine, jnp.zeros((tail - groups, LANES), jnp.float32)], axis=0)
        out_ref[part, 2 * channels :, :] = block.astype(jnp.bfloat16)


def widen_blocks(blocks_ref, first, wide_ref):
    for part in range(blocks_ref.shape[0]):
        row = (part // 2) * GROUP
        lane = (part % 2) * LANES
        wide_ref[row : row + GROUP, lane : lane + LANES] = blocks_ref[
            part, pl.ds(first, GROUP), :
        ]


def input_kernel(blocks_ref, out_ref, line_ref, wide_ref, toep_ref):
    parts, channels, _ = out_ref.shape
    groups = channels // GROUP
    half = parts // 2
    rows = half * GROUP
    wide_ref[rows:, :] = jnp.zeros_like(wide_ref[rows:, :])
    line_ref[...] = jnp.zeros_like(line_ref)
    for part in range(parts):
        start = (part + 1) * LANES
        line_ref[:, start : start + LANES] = blocks_ref[part, 2 * channels :, :][
            : line_ref.shape[0]
        ].astype(jnp.float32)

    def per_group(group, carry):
        first = pl.multiple_of(group * GROUP, GROUP)
        widen_blocks(blocks_ref, first, wide_ref)
        line = line_ref[pl.ds(group, 1), :]
        spread = jnp.broadcast_to(line, (LANES, line.shape[1]))
        toep_ref[...] = pltpu.roll(spread, 0, 1, stride=1, stride_axis=0).astype(jnp.bfloat16)
        total = jnp.zeros((rows, SPAN), jnp.float32)
        for lag in range(half):
            start = lag * SPAN
            taps = jnp.concatenate(
                [
                    toep_ref[:, start + LANES : start + LANES + SPAN],
                    toep_ref[:, start : start + SPAN],
                ],
                axis=0,
            )
            total = total + lax.dot_general(
                wide_ref[lag * GROUP : lag * GROUP + rows, :],
                taps,
                (((1,), (1,)), ((), ())),
                preferred_element_type=jnp.float32,
            )
        done = total.astype(jnp.bfloat16)
        for part in range(parts):
            row = (part // 2) * GROUP
            lane = (part % 2) * LANES
            out_ref[part, pl.ds(first, GROUP), :] = done[
                row : row + GROUP, lane : lane + LANES
            ]
        return carry

    lax.fori_loop(0, groups, per_group, 0)


def filter_kernel(side_of, blocks_ref, *refs):
    out_refs, (wide_ref, saved_wide_ref, toep_ref, sums_ref) = refs[:SIDE], refs[SIDE:]
    parts, rows_all, _ = blocks_ref.shape
    half = parts // 2
    rows = half * GROUP
    groups = sums_ref.shape[1]
    channels = groups * GROUP
    wide_ref[rows:, :] = jnp.zeros_like(wide_ref[rows:, :])
    row_ids = lax.broadcasted_iota(jnp.int32, (SPAN, SPAN), 0)
    col_ids = lax.broadcasted_iota(jnp.int32, (SPAN, SPAN), 1)
    mirror = (row_ids // LANES) * LANES + (LANES - 1 - row_ids % LANES)
    flip = jnp.where(mirror == col_ids, 1.0, 0.0).astype(jnp.bfloat16)

    def per_group(group, carry):
        first = pl.multiple_of(group * GROUP, GROUP)
        widen_blocks(blocks_ref, first, wide_ref)
        widen_blocks(blocks_ref, first + channels, saved_wide_ref)
        saved_lag = lax.dot_general(
            flip,
            saved_wide_ref[...],
            (((1,), (1,)), ((), ())),
            preferred_element_type=jnp.float32,
        ).astype(jnp.bfloat16)
        toep_ref[...] = jnp.zeros_like(toep_ref)
        for lag in range(half):
            start = lag * SPAN
            piece = jnp.dot(
                saved_lag,
                wide_ref[lag * GROUP : lag * GROUP + rows, :],
                preferred_element_type=jnp.float32,
            )
            toep_ref[:, start + LANES : start + LANES + SPAN] += piece[:LANES, :]
            toep_ref[:, start : start + SPAN] += piece[LANES:, :]
        turned = pltpu.roll(toep_ref[...], 1, 1, stride=1, stride_axis=0)
        line = jnp.sum(turned, axis=0, keepdims=True)
        for part in range(parts):
            start = SPAN + part * LANES
            sums_ref[part, pl.ds(group, 1), :] = line[:, start : start + LANES]
        return carry

    lax.fori_loop(0, groups, per_group, 0)
    share = parts // SIDE
    side = side_of()
    for step in range(SIDE):
        first = lax.rem(side + step, SIDE) * share
        out_refs[step][...] = sums_ref[pl.ds(first, share)]


def join_kernel(side_of, *refs):
    in_refs, out_refs = refs[:SIDE], refs[SIDE:]
    count = len(out_refs)
    total = in_refs[0][...] + in_refs[1][...] + in_refs[2][...] + in_refs[3][...]
    share = total.shape[0] // count
    side = side_of()
    for step in range(count):
        place = lax.rem(side + step, count)
        value = total[:share]
        for other in range(1, count):
            value = jnp.where(place == other, total[other * share : (other + 1) * share], value)
        out_refs[step][...] = value


def last_kernel(side_of, scale, near_ref, far_ref, out_ref):
    near, far = near_ref[0] * scale, far_ref[0] * scale
    even = side_of() == 0
    first = jnp.where(even, near, far)
    second = jnp.where(even, far, near)
    out_ref[...] = jnp.concatenate([first, second], axis=0)


def shifted(step, stride):
    moves = []
    for device in range(SIDE * SIDE):
        place = device // stride % SIDE
        moves.append((device, device + ((place + step) % SIDE - place) * stride))
    return moves


def on_device(u_saved, grad_out, filters):
    parts = lax.axis_size("ctx")
    seqs = lax.axis_size("dp")
    channels = u_saved.shape[2] // parts
    groups = channels // GROUP
    length = parts * LANES
    bf16, f32 = jnp.bfloat16, jnp.float32
    half_rows = parts // 2 * GROUP

    packed = call(
        pack_kernel,
        jax.ShapeDtypeStruct((parts, 2 * channels + 8, LANES), bf16),
        u_saved[0],
        grad_out[0],
        filters,
        vmem=8 * MIB,
    )
    blocks = lax.all_to_all(packed, "ctx", split_axis=0, concat_axis=0, tiled=True)
    input_blocks = call(
        input_kernel,
        jax.ShapeDtypeStruct((parts, channels, LANES), bf16),
        blocks,
        scratch=[
            pltpu.VMEM((groups, length + SPAN), f32),
            pltpu.VMEM((2 * half_rows, SPAN), bf16),
            pltpu.VMEM((LANES, length + SPAN), bf16),
        ],
        flops=2**31,
        vmem=20 * MIB,
    )
    returned = lax.all_to_all(input_blocks, "ctx", split_axis=0, concat_axis=0, tiled=True)

    def slow_side():
        return lax.axis_index("dp") // SIDE

    def fast_side():
        return lax.rem(lax.axis_index("dp"), SIDE)

    def parity():
        return lax.rem(lax.axis_index("ctx"), 2)

    shares = call(
        lambda *refs: filter_kernel(slow_side, *refs),
        [jax.ShapeDtypeStruct((parts // SIDE, groups, LANES), f32)] * SIDE,
        blocks,
        scratch=[
            pltpu.VMEM((2 * half_rows, SPAN), bf16),
            pltpu.VMEM((half_rows, SPAN), bf16),
            pltpu.VMEM((LANES, length + SPAN), f32),
            pltpu.VMEM((parts, groups, LANES), f32),
        ],
        flops=2**31,
        vmem=20 * MIB,
    )
    came = [shares[0]] + [
        lax.ppermute(shares[step], "dp", shifted(step, SIDE)) for step in range(1, SIDE)
    ]
    shares = call(
        lambda *refs: join_kernel(fast_side, *refs),
        [jax.ShapeDtypeStruct((parts // SIDE**2, groups, LANES), f32)] * SIDE,
        *came,
    )
    came = [shares[0]] + [
        lax.ppermute(shares[step], "dp", shifted(step, 1)) for step in range(1, SIDE)
    ]
    near, far = call(
        lambda *refs: join_kernel(parity, *refs),
        [jax.ShapeDtypeStruct((1, groups, LANES), f32)] * 2,
        *came,
    )
    near_moves, far_moves = [], []
    for seq in range(seqs):
        for part in range(parts):
            here = seq * parts + part
            base = (part // 2) * parts + 2 * seq
            near_moves.append((here, base + part % 2))
            far_moves.append((here, base + 1 - part % 2))
    near = lax.ppermute(near, ("dp", "ctx"), near_moves)
    far = lax.ppermute(far, ("dp", "ctx"), far_moves)
    scale = 1.0 / math.sqrt(GROUP * seqs * length)
    filter_part = call(
        lambda *refs: last_kernel(parity, scale, *refs),
        jax.ShapeDtypeStruct((2 * groups, LANES), f32),
        near,
        far,
    )
    input_grad = returned.reshape(-1, LANES).T[None]
    return (input_grad, filter_part.T)


def solution(mesh):
    in_specs = (P("dp", "ctx", None), P("dp", "ctx", None), P("ctx", None))
    out_specs = (P("dp", "ctx", None), P("ctx", "dp"))
    return jax.shard_map(
        on_device, mesh=mesh, in_specs=in_specs, out_specs=out_specs, check_vma=False
    )
```

time: 274 us -> 116 us (0.42)
  the two profiles are of different devices: /device:TPU:8 before, /device:TPU:12 now
where the time goes in v1:
time: 116 us; the launch traced here: 115 us
  starting transfers between devices  44.3 us (38%)
  blocking collectives  39.4 us (34%)
  waiting for transfers between devices  17 us (15%)
  Pallas kernels  9.63 us (8%)
  local copies, waits for them, and re-layouts  3.84 us (3%)
    all_to_all x1, blocking collectives, on_device(): lax.all_to_all(packed, 'ctx', split_axis=0, concat_axis=0, tiled=True)  39.4 us
    ppermute x3, starting transfers between devices, on_device(): lax.ppermute(shares[step], 'dp', shifted(step, 1))  17.9 us
    pallas_call x6, Pallas kernels, call(): pl.pallas_call(kernel, out_shape=out_shape, in_specs=[in_vmem] * len(oper...  9.63 us
    ppermute x1, starting transfers between devices, on_device(): near = lax.ppermute(near, ('dp', 'ctx'), near_moves)  9.23 us
    ppermute x3, starting transfers between devices, on_device(): lax.ppermute(shares[step], 'dp', shifted(step, SIDE))  8.88 us
    ppermute x1, waiting for transfers between devices, on_device(): far = lax.ppermute(far, ('dp', 'ctx'), far_moves)  8.66 us
    all_to_all x1, starting transfers between devices, on_device(): lax.all_to_all(input_blocks, 'ctx', split_axis=0, concat_axis=0, tiled=True)  4.82 us
    ppermute x1, starting transfers between devices, on_device(): far = lax.ppermute(far, ('dp', 'ctx'), far_moves)  3.46 us
  transfers between devices with their start and end apart: 9, of which 5 were waited for; matrix products, arithmetic and copies ran while one was open for 0% of the time, Pallas kernels for 4%

profile of v1, /device:TPU:12, one launch (start us, length us, event | category | flops | bytes accessed | tf_op | source)
XLA Modules:
  0.0 115.0 jit_solution(12898910927464045981)
XLA Ops:
  0.6 1.0 copy-done
  1.7 1.0 copy-done.1
  2.7 0.8 copy-done.2
  3.5 0.4 shard_map.50
  3.8 39.4 %all_to_all.10.blocks_ref.refs_0_ = bf16[32,136,128]{2,1,0:T(8,128)(2,1)S(1)} all-to-all(bf16[32,136,128]{2,1,0:T(8,128)(2,1)S(1)} %shard_map.50), channel_id=1, replica_groups=mesh['dp'=16,'ctx'=32] {'ctx'}, dimensions={0} | all-to-all | bytes 2228224 | tf_op jit(solution)/shard_map/all_to_all | solution.py:204
  43.2 4.4 %shard_map.51 = bf16[32,64,128]{2,1,0:T(8,128)(2,1)} custom-call(bf16[32,136,128]{2,1,0:T(8,128)(2,1)S(1)} %all_to_all.10.blocks_ref.refs_0_), custom_call_target="tpu_custom_call" | custom-call | flops 2147483648 | bytes 1048576 | tf_op jit(solution)/shard_map/pallas_call | solution.py:20
  47.7 4.8 %all-to-all-start.1 = ((bf16[32,64,128]{2,1,0:T(8,128)(2,1)}), bf16[32,64,128]{2,1,0:T(8,128)(2,1)S(1)}, u32[]{:S(2)}, u32[]{:S(2)}) async-start(bf16[32,64,128]{2,1,0:T(8,128)(2,1)} %shard_map.51), calls=%async_computation.1 | async-start | bytes 1048576 | tf_op jit(solution)/shard_map/all_to_all | solution.py:217
  52.5 4.2 %shard_map.52 = (f32[8,4,128]{2,1,0:T(4,128)S(1)}, f32[8,4,128]{2,1,0:T(4,128)S(1)}, f32[8,4,128]{2,1,0:T(4,128)S(1)}, f32[8,4,128]{2,1,0:T(4,128)S(1)}) custom-call(bf16[32,136,128]{2,1,0:T(8,128)(2,1)S(1)} %all_to_all.10.blocks_ref.refs_0_), custom_call_target="tpu_custom_call" | custom-call | flops 2147483648 | bytes 1048576 | tf_op jit(solution)/shard_map/pallas_call | solution.py:20
  56.7 3.1 %collective-permute-start = (f32[8,4,128]{2,1,0:T(4,128)S(1)}, f32[8,4,128]{2,1,0:T(4,128)S(1)}, u32[]{:S(2)}, u32[]{:S(2)}) collective-permute-start(f32[8,4,128]{2,1,0:T(4,128)S(1)} %get-tuple-element.13), channel_id=1, source_target_pairs={{0,128},{32,160},{64,192},{96,224},{128,256},{160,288},{192,320},{... | collective-permute-start | bytes 49160 | tf_op jit(solution)/shard_map/ppermute | solution.py:242
  59.8 2.7 %collective-permute-start.1 = (f32[8,4,128]{2,1,0:T(4,128)S(1)}, f32[8,4,128]{2,1,0:T(4,128)S(1)}, u32[]{:S(2)}, u32[]{:S(2)}) collective-permute-start(f32[8,4,128]{2,1,0:T(4,128)S(1)} %get-tuple-element.14), channel_id=1, source_target_pairs={{0,256},{32,288},{64,320},{96,352},{128,384},{160,416},{192,448},{... | collective-permute-start | bytes 49160 | tf_op jit(solution)/shard_map/ppermute | solution.py:242
  62.5 3.1 %collective-permute-start.2 = (f32[8,4,128]{2,1,0:T(4,128)S(1)}, f32[8,4,128]{2,1,0:T(4,128)S(1)}, u32[]{:S(2)}, u32[]{:S(2)}) collective-permute-start(f32[8,4,128]{2,1,0:T(4,128)S(1)} %get-tuple-element.15), channel_id=1, source_target_pairs={{0,384},{32,416},{64,448},{96,480},{128,0},{160,32},{192,64},{224,... | collective-permute-start | bytes 49160 | tf_op jit(solution)/shard_map/ppermute | solution.py:242
  65.6 0.0 collective-permute-done.refs_1_
  65.6 1.3 %collective-permute-done.1.refs_2_ = f32[8,4,128]{2,1,0:T(4,128)S(1)} collective-permute-done((f32[8,4,128]{2,1,0:T(4,128)S(1)}, f32[8,4,128]{2,1,0:T(4,128)S(1)}, u32[]{:S(2)}, u32[]{:S(2)}) %collective-permute-start.1) | collective-permute-done | bytes 16416 | tf_op jit(solution)/shard_map/ppermute | solution.py:242
  67.0 1.3 %collective-permute-done.2.refs_3_ = f32[8,4,128]{2,1,0:T(4,128)S(1)} collective-permute-done((f32[8,4,128]{2,1,0:T(4,128)S(1)}, f32[8,4,128]{2,1,0:T(4,128)S(1)}, u32[]{:S(2)}, u32[]{:S(2)}) %collective-permute-start.2) | collective-permute-done | bytes 16416 | tf_op jit(solution)/shard_map/ppermute | solution.py:242
  68.3 6.0 %collective-permute-start.3 = (f32[2,4,128]{2,1,0:T(4,128)S(1)}, f32[2,4,128]{2,1,0:T(4,128)S(1)}, u32[]{:S(2)}, u32[]{:S(2)}) collective-permute-start(f32[2,4,128]{2,1,0:T(4,128)S(1)} %get-tuple-element.17), channel_id=1, source_target_pairs={{0,32},{32,64},{64,96},{96,0},{128,160},{160,192},{192,224},{224,1... | collective-permute-start | bytes 12296 | tf_op jit(solution)/shard_map/ppermute | solution.py:250
  74.4 8.2 %collective-permute-start.4 = (f32[2,4,128]{2,1,0:T(4,128)S(1)}, f32[2,4,128]{2,1,0:T(4,128)S(1)}, u32[]{:S(2)}, u32[]{:S(2)}) collective-permute-start(f32[2,4,128]{2,1,0:T(4,128)S(1)} %get-tuple-element.18), channel_id=1, source_target_pairs={{0,64},{32,96},{64,0},{96,32},{128,192},{160,224},{192,128},{224,1... | collective-permute-start | bytes 12296 | tf_op jit(solution)/shard_map/ppermute | solution.py:250
  82.6 3.7 %collective-permute-start.5 = (f32[2,4,128]{2,1,0:T(4,128)S(1)}, f32[2,4,128]{2,1,0:T(4,128)S(1)}, u32[]{:S(2)}, u32[]{:S(2)}) collective-permute-start(f32[2,4,128]{2,1,0:T(4,128)S(1)} %get-tuple-element.19), channel_id=1, source_target_pairs={{0,96},{32,0},{64,32},{96,64},{128,224},{160,128},{192,160},{224,1... | collective-permute-start | bytes 12296 | tf_op jit(solution)/shard_map/ppermute | solution.py:250
  86.3 2.7 %collective-permute-done.5.refs_3_ = f32[2,4,128]{2,1,0:T(4,128)S(1)} collective-permute-done((f32[2,4,128]{2,1,0:T(4,128)S(1)}, f32[2,4,128]{2,1,0:T(4,128)S(1)}, u32[]{:S(2)}, u32[]{:S(2)}) %collective-permute-start.5) | collective-permute-done | bytes 4128 | tf_op jit(solution)/shard_map/ppermute | solution.py:250
  89.0 9.2 %collective-permute-start.6 = (f32[1,4,128]{2,1,0:T(4,128)S(1)}, f32[1,4,128]{2,1,0:T(4,128)S(1)}, u32[]{:S(2)}, u32[]{:S(2)}) collective-permute-start(f32[1,4,128]{2,1,0:T(4,128)S(1)} %get-tuple-element.20), channel_id=1, source_target_pairs={{0,0},{1,1},{2,32},{3,33},{4,64},{5,65},{6,96},{7,97},{8,128},{9,1... | collective-permute-start | bytes 6152 | tf_op jit(solution)/shard_map/ppermute | solution.py:264
  98.2 3.5 %collective-permute-start.7 = (f32[1,4,128]{2,1,0:T(4,128)S(1)}, f32[1,4,128]{2,1,0:T(4,128)S(1)}, u32[]{:S(2)}, u32[]{:S(2)}) collective-permute-start(f32[1,4,128]{2,1,0:T(4,128)S(1)} %get-tuple-element.21), channel_id=1, source_target_pairs={{0,1},{1,0},{2,33},{3,32},{4,65},{5,64},{6,97},{7,96},{8,129},{9,1... | collective-permute-start | bytes 6152 | tf_op jit(solution)/shard_map/ppermute | solution.py:265
  101.7 3.0 %collective-permute-done.6.refs_0_ = f32[1,4,128]{2,1,0:T(4,128)S(1)} collective-permute-done((f32[1,4,128]{2,1,0:T(4,128)S(1)}, f32[1,4,128]{2,1,0:T(4,128)S(1)}, u32[]{:S(2)}, u32[]{:S(2)}) %collective-permute-start.6) | collective-permute-done | bytes 2080 | tf_op jit(solution)/shard_map/ppermute | solution.py:264
  104.7 8.7 %collective-permute-done.7.refs_1_ = f32[1,4,128]{2,1,0:T(4,128)S(1)} collective-permute-done((f32[1,4,128]{2,1,0:T(4,128)S(1)}, f32[1,4,128]{2,1,0:T(4,128)S(1)}, u32[]{:S(2)}, u32[]{:S(2)}) %collective-permute-start.7) | collective-permute-done | bytes 2080 | tf_op jit(solution)/shard_map/ppermute | solution.py:265
  113.3 0.6 shard_map.55
  113.9 1.0 copy.5
  (8 shorter events, 0.0 us)
Async XLA Ops:
  0.6 1.0 copy-start
  1.7 1.0 copy-start.1
  2.7 0.8 copy-start.2
  47.7 66.3 %all-to-all-start.1 = ((bf16[32,64,128]{2,1,0:T(8,128)(2,1)}), bf16[32,64,128]{2,1,0:T(8,128)(2,1)S(1)}, u32[]{:S(2)}, u32[]{:S(2)}) async-start(bf16[32,64,128]{2,1,0:T(8,128)(2,1)} %shard_map.51), calls=%async_computation.1 | async-start | bytes 1048576 | tf_op jit(solution)/shard_map/all_to_all | solution.py:217
  56.7 8.9 %collective-permute-start = (f32[8,4,128]{2,1,0:T(4,128)S(1)}, f32[8,4,128]{2,1,0:T(4,128)S(1)}, u32[]{:S(2)}, u32[]{:S(2)}) collective-permute-start(f32[8,4,128]{2,1,0:T(4,128)S(1)} %get-tuple-element.13), channel_id=1, source_target_pairs={{0,128},{32,160},{64,192},{96,224},{128,256},{160,288},{192,320},{... | collective-permute-start | bytes 49160 | tf_op jit(solution)/shard_map/ppermute | solution.py:242
  59.8 7.1 %collective-permute-start.1 = (f32[8,4,128]{2,1,0:T(4,128)S(1)}, f32[8,4,128]{2,1,0:T(4,128)S(1)}, u32[]{:S(2)}, u32[]{:S(2)}) collective-permute-start(f32[8,4,128]{2,1,0:T(4,128)S(1)} %get-tuple-element.14), channel_id=1, source_target_pairs={{0,256},{32,288},{64,320},{96,352},{128,384},{160,416},{192,448},{... | collective-permute-start | bytes 49160 | tf_op jit(solution)/shard_map/ppermute | solution.py:242
  62.5 5.8 %collective-permute-start.2 = (f32[8,4,128]{2,1,0:T(4,128)S(1)}, f32[8,4,128]{2,1,0:T(4,128)S(1)}, u32[]{:S(2)}, u32[]{:S(2)}) collective-permute-start(f32[8,4,128]{2,1,0:T(4,128)S(1)} %get-tuple-element.15), channel_id=1, source_target_pairs={{0,384},{32,416},{64,448},{96,480},{128,0},{160,32},{192,64},{224,... | collective-permute-start | bytes 49160 | tf_op jit(solution)/shard_map/ppermute | solution.py:242
  68.3 17.9 %collective-permute-start.3 = (f32[2,4,128]{2,1,0:T(4,128)S(1)}, f32[2,4,128]{2,1,0:T(4,128)S(1)}, u32[]{:S(2)}, u32[]{:S(2)}) collective-permute-start(f32[2,4,128]{2,1,0:T(4,128)S(1)} %get-tuple-element.17), channel_id=1, source_target_pairs={{0,32},{32,64},{64,96},{96,0},{128,160},{160,192},{192,224},{224,1... | collective-permute-start | bytes 12296 | tf_op jit(solution)/shard_map/ppermute | solution.py:250
  74.4 11.9 %collective-permute-start.4 = (f32[2,4,128]{2,1,0:T(4,128)S(1)}, f32[2,4,128]{2,1,0:T(4,128)S(1)}, u32[]{:S(2)}, u32[]{:S(2)}) collective-permute-start(f32[2,4,128]{2,1,0:T(4,128)S(1)} %get-tuple-element.18), channel_id=1, source_target_pairs={{0,64},{32,96},{64,0},{96,32},{128,192},{160,224},{192,128},{224,1... | collective-permute-start | bytes 12296 | tf_op jit(solution)/shard_map/ppermute | solution.py:250
  82.6 6.4 %collective-permute-start.5 = (f32[2,4,128]{2,1,0:T(4,128)S(1)}, f32[2,4,128]{2,1,0:T(4,128)S(1)}, u32[]{:S(2)}, u32[]{:S(2)}) collective-permute-start(f32[2,4,128]{2,1,0:T(4,128)S(1)} %get-tuple-element.19), channel_id=1, source_target_pairs={{0,96},{32,0},{64,32},{96,64},{128,224},{160,128},{192,160},{224,1... | collective-permute-start | bytes 12296 | tf_op jit(solution)/shard_map/ppermute | solution.py:250
  89.0 15.7 %collective-permute-start.6 = (f32[1,4,128]{2,1,0:T(4,128)S(1)}, f32[1,4,128]{2,1,0:T(4,128)S(1)}, u32[]{:S(2)}, u32[]{:S(2)}) collective-permute-start(f32[1,4,128]{2,1,0:T(4,128)S(1)} %get-tuple-element.20), channel_id=1, source_target_pairs={{0,0},{1,1},{2,32},{3,33},{4,64},{5,65},{6,96},{7,97},{8,128},{9,1... | collective-permute-start | bytes 6152 | tf_op jit(solution)/shard_map/ppermute | solution.py:264
  98.2 15.1 %collective-permute-start.7 = (f32[1,4,128]{2,1,0:T(4,128)S(1)}, f32[1,4,128]{2,1,0:T(4,128)S(1)}, u32[]{:S(2)}, u32[]{:S(2)}) collective-permute-start(f32[1,4,128]{2,1,0:T(4,128)S(1)} %get-tuple-element.21), channel_id=1, source_target_pairs={{0,1},{1,0},{2,33},{3,32},{4,65},{5,64},{6,97},{7,96},{8,129},{9,1... | collective-permute-start | bytes 6152 | tf_op jit(solution)/shard_map/ppermute | solution.py:265

commit v2 on v1

v2 whole, which is shorter than its diff:
```python
import math

import jax
import jax.numpy as jnp
from jax import lax
from jax.experimental import pallas as pl
from jax.experimental.pallas import tpu as pltpu
from jax.sharding import Mesh, PartitionSpec as P

GROUP = 16
LANES = 128
SPAN = 2 * LANES
SIDE = 4
MIB = 1024 * 1024
PACK_VMEM = 8 * MIB


def call(kernel, out_shape, *operands, scratch=(), flops=2**20, vmem=2 * MIB):
    in_vmem = pl.BlockSpec(memory_space=pltpu.VMEM)
    several = isinstance(out_shape, (list, tuple))
    return pl.pallas_call(
        kernel,
        out_shape=out_shape,
        in_specs=[in_vmem] * len(operands),
        out_specs=[in_vmem] * len(out_shape) if several else in_vmem,
        scratch_shapes=list(scratch),
        compiler_params=pltpu.CompilerParams(vmem_limit_bytes=vmem),
        cost_estimate=pl.CostEstimate(flops=flops, bytes_accessed=2**20, transcendentals=0),
    )(*operands)


def pack_kernel(saved_ref, grad_ref, filt_ref, out_ref, lines_ref):
    places, groups = LANES // GROUP, SIDE
    channels = groups * GROUP
    for tile in range(groups * SIDE):
        slot, inner = tile // SIDE, tile % SIDE
        cols = slice(tile * LANES, (tile + 1) * LANES)
        grad_rows = grad_ref[:, cols].T
        saved_rows = saved_ref[:, cols].T
        for place in range(places):
            part = place * SIDE + inner
            mine = slice(place * GROUP, (place + 1) * GROUP)
            row = slot * GROUP
            out_ref[part, row : row + GROUP, :] = grad_rows[mine, :]
            out_ref[part, channels + row : channels + row + GROUP, :] = saved_rows[mine, :]
    lines_ref[...] = filt_ref[...].astype(jnp.float32).T
    empty = jnp.zeros((out_ref.shape[1] - 2 * channels - groups, LANES), jnp.float32)
    for place in range(places):
        for inner in range(SIDE):
            first = inner * places + place
            mine = lines_ref[pl.ds(first, groups, stride=SIDE * places), :]
            block = jnp.concatenate([mine, empty], axis=0)
            out_ref[place * SIDE + inner, 2 * channels :, :] = block.astype(jnp.bfloat16)


def unpack_kernel(blocks_ref, out_ref):
    places = LANES // GROUP
    for tile in range(out_ref.shape[1] // LANES):
        slot, inner = tile // SIDE, tile % SIDE
        row = slot * GROUP
        rows = [
            blocks_ref[place * SIDE + inner, row : row + GROUP, :] for place in range(places)
        ]
        out_ref[:, tile * LANES : (tile + 1) * LANES] = jnp.concatenate(rows, axis=0).T


def widen_blocks(blocks_ref, first, wide_ref):
    for part in range(blocks_ref.shape[0]):
        row = (part // 2) * GROUP
        lane = (part % 2) * LANES
        wide_ref[row : row + GROUP, lane : lane + LANES] = blocks_ref[
            part, pl.ds(first, GROUP), :
        ]


def input_kernel(blocks_ref, out_ref, line_ref, wide_ref, toep_ref):
    parts, channels, _ = out_ref.shape
    groups = channels // GROUP
    half = parts // 2
    rows = half * GROUP
    wide_ref[rows:, :] = jnp.zeros_like(wide_ref[rows:, :])
    line_ref[...] = jnp.zeros_like(line_ref)
    for part in range(parts):
        start = (part + 1) * LANES
        line_ref[:, start : start + LANES] = blocks_ref[part, 2 * channels :, :][
            : line_ref.shape[0]
        ].astype(jnp.float32)

    def per_group(group, carry):
        first = pl.multiple_of(group * GROUP, GROUP)
        widen_blocks(blocks_ref, first, wide_ref)
        line = line_ref[pl.ds(group, 1), :]
        spread = jnp.broadcast_to(line, (LANES, line.shape[1]))
        toep_ref[...] = pltpu.roll(spread, 0, 1, stride=1, stride_axis=0).astype(jnp.bfloat16)
        total = jnp.zeros((rows, SPAN), jnp.float32)
        for lag in range(half):
            start = lag * SPAN
            taps = jnp.concatenate(
                [
                    toep_ref[:, start + LANES : start + LANES + SPAN],
                    toep_ref[:, start : start + SPAN],
                ],
                axis=0,
            )
            total = total + lax.dot_general(
                wide_ref[lag * GROUP : lag * GROUP + rows, :],
                taps,
                (((1,), (1,)), ((), ())),
                preferred_element_type=jnp.float32,
            )
        done = total.astype(jnp.bfloat16)
        for part in range(parts):
            row = (part // 2) * GROUP
            lane = (part % 2) * LANES
            out_ref[part, pl.ds(first, GROUP), :] = done[
                row : row + GROUP, lane : lane + LANES
            ]
        return carry

    lax.fori_loop(0, groups, per_group, 0)


def filter_kernel(blocks_ref, out_ref, wide_ref, saved_wide_ref, toep_ref):
    parts, _, _ = blocks_ref.shape
    half = parts // 2
    rows = half * GROUP
    groups = SIDE
    places = parts // SIDE
    channels = groups * GROUP
    wide_ref[rows:, :] = jnp.zeros_like(wide_ref[rows:, :])
    row_ids = lax.broadcasted_iota(jnp.int32, (SPAN, SPAN), 0)
    col_ids = lax.broadcasted_iota(jnp.int32, (SPAN, SPAN), 1)
    mirror = (row_ids // LANES) * LANES + (LANES - 1 - row_ids % LANES)
    flip = jnp.where(mirror == col_ids, 1.0, 0.0).astype(jnp.bfloat16)

    def per_group(group, carry):
        first = pl.multiple_of(group * GROUP, GROUP)
        widen_blocks(blocks_ref, first, wide_ref)
        widen_blocks(blocks_ref, first + channels, saved_wide_ref)
        saved_lag = lax.dot_general(
            flip,
            saved_wide_ref[...],
            (((1,), (1,)), ((), ())),
            preferred_element_type=jnp.float32,
        ).astype(jnp.bfloat16)
        toep_ref[...] = jnp.zeros_like(toep_ref)
        for lag in range(half):
            start = lag * SPAN
            piece = jnp.dot(
                saved_lag,
                wide_ref[lag * GROUP : lag * GROUP + rows, :],
                preferred_element_type=jnp.float32,
            )
            toep_ref[:, start + LANES : start + LANES + SPAN] += piece[:LANES, :]
            toep_ref[:, start : start + SPAN] += piece[LANES:, :]
        turned = pltpu.roll(toep_ref[...], 1, 1, stride=1, stride_axis=0)
        line = jnp.sum(turned, axis=0, keepdims=True)
        for part in range(parts):
            start = SPAN + part * LANES
            inner = part % SIDE
            out_ref[group * places + part // SIDE, inner : inner + 1, :] = line[
                :, start : start + LANES
            ]
        return carry

    lax.fori_loop(0, groups, per_group, 0)


def join_kernel(came_ref, *out_refs):
    places = came_ref.shape[0] // SIDE
    total = came_ref[:places]
    for step in range(1, SIDE):
        total = total + came_ref[step * places : (step + 1) * places]
    side = lax.axis_index("zh")
    for step in range(SIDE):
        inner = lax.rem(side + step, SIDE)
        value = total[:, 0, :]
        for other in range(1, SIDE):
            value = jnp.where(inner == other, total[:, other, :], value)
        out_refs[step][...] = value


def last_kernel(scale, *refs):
    in_refs, out_ref = refs[:SIDE], refs[SIDE]
    total = in_refs[0][...] + in_refs[1][...] + in_refs[2][...] + in_refs[3][...]
    out_ref[...] = total * scale


def on_device(u_saved, grad_out, filters):
    tokens, width = u_saved.shape[1:]
    parts = lax.axis_size(("y", "w"))
    seqs = lax.axis_size(("x", "zh"))
    places = lax.axis_size("y")
    channels = width // parts
    groups = channels // GROUP
    length = parts * LANES
    bf16, f32 = jnp.bfloat16, jnp.float32
    half_rows = parts // 2 * GROUP

    packed = call(
        pack_kernel,
        jax.ShapeDtypeStruct((parts, 2 * channels + 8, LANES), bf16),
        u_saved[0],
        grad_out[0],
        filters,
        scratch=[pltpu.VMEM((LANES, LANES), f32)],
        vmem=PACK_VMEM,
    )
    blocks = lax.all_to_all(packed, ("y", "w"), split_axis=0, concat_axis=0, tiled=True)
    lags = call(
        filter_kernel,
        jax.ShapeDtypeStruct((parts, SIDE, LANES), f32),
        blocks,
        scratch=[
            pltpu.VMEM((2 * half_rows, SPAN), bf16),
            pltpu.VMEM((half_rows, SPAN), bf16),
            pltpu.VMEM((LANES, length + SPAN), f32),
        ],
        flops=2**31,
        vmem=20 * MIB,
    )
    lags_came = lax.all_to_all(lags, ("x", "y"), split_axis=0, concat_axis=0, tiled=True)
    input_blocks = call(
        input_kernel,
        jax.ShapeDtypeStruct((parts, channels, LANES), bf16),
        blocks,
        scratch=[
            pltpu.VMEM((groups, length + SPAN), f32),
            pltpu.VMEM((2 * half_rows, SPAN), bf16),
            pltpu.VMEM((LANES, length + SPAN), bf16),
        ],
        flops=2**31,
        vmem=20 * MIB,
    )
    input_blocks, lags_came = lax.optimization_barrier((input_blocks, lags_came))
    returned = lax.all_to_all(input_blocks, ("y", "w"), split_axis=0, concat_axis=0, tiled=True)
    shares = call(
        join_kernel,
        [jax.ShapeDtypeStruct((places, LANES), f32)] * SIDE,
        lags_came,
    )
    came = []
    for step in range(SIDE):
        moves = []
        for side in range(SIDE):
            for inner in range(SIDE):
                moves.append((side * SIDE + inner, inner * SIDE + (side + step) % SIDE))
        came.append(lax.ppermute(shares[step], ("zh", "w"), moves))
    scale = 1.0 / math.sqrt(GROUP * seqs * length)
    filter_part = call(
        lambda *refs: last_kernel(scale, *refs),
        jax.ShapeDtypeStruct((places, LANES), f32),
        *came,
    )
    input_grad = call(
        unpack_kernel, jax.ShapeDtypeStruct((tokens, width), bf16), returned, vmem=4 * MIB
    )
    return (input_grad[None], filter_part.T)


def solution(mesh):
    cut = Mesh(mesh.devices.reshape(SIDE, SIDE, -1, SIDE), ("x", "zh", "y", "w"))
    seq, token = ("x", "zh"), ("y", "w")
    in_specs = (P(seq, token, None), P(seq, token, None), P(token, None))
    out_specs = (P(seq, token, None), P(token, seq))
    return jax.shard_map(
        on_device, mesh=cut, in_specs=in_specs, out_specs=out_specs, check_vma=False
    )
```

time: 116 us -> 94.4 us (0.81)
  the two profiles are of different devices: /device:TPU:12 before, /device:TPU:1 now
where the time goes in v2:
time: 94.4 us; the launch traced here: 93.9 us
  blocking collectives  40.7 us (43%)
  starting transfers between devices  30.1 us (32%)
  Pallas kernels  11.3 us (12%)
  waiting for transfers between devices  8.24 us (9%)
  local copies, waits for them, and re-layouts  2.83 us (3%)
    all_to_all x1, blocking collectives, on_device(): lax.all_to_all(packed, ('y', 'w'), split_axis=0, concat_axis=0, tiled=True)  40.7 us
    ppermute x4, starting transfers between devices, on_device(): came.append(lax.ppermute(shares[step], ('zh', 'w'), moves))  19.2 us
    pallas_call x6, Pallas kernels, call(): pl.pallas_call(kernel, out_shape=out_shape, in_specs=[in_vmem] * len(oper...  11.3 us
    all_to_all x1, starting transfers between devices, on_device(): lax.all_to_all(input_blocks, ('y', 'w'), split_axis=0, concat_axis=0, til...  5.47 us
    all_to_all x1, starting transfers between devices, on_device(): lax.all_to_all(lags, ('x', 'y'), split_axis=0, concat_axis=0, tiled=True)  5.36 us
    all_to_all x1, waiting for transfers between devices, on_device(): lax.all_to_all(lags, ('x', 'y'), split_axis=0, concat_axis=0, tiled=True)  4.41 us
    ppermute x4, waiting for transfers between devices, on_device(): came.append(lax.ppermute(shares[step], ('zh', 'w'), moves))  3.83 us
    unnamed x6, local copies, waits for them, and re-layouts  2.83 us
  transfers between devices with their start and end apart: 6, of which 2 were waited for; matrix products, arithmetic and copies ran while one was open for 0% of the time, Pallas kernels for 5%

profile of v2, /device:TPU:1, one launch (start us, length us, event | category | flops | bytes accessed | tf_op | source)
XLA Modules:
  0.0 93.9 jit_solution(14106428465959136357)
XLA Ops:
  0.6 0.0 copy-start
  0.6 1.0 %copy-done = bf16[1,128,2048]{2,1,0:T(8,128)(2,1)S(1)} copy-done((bf16[1,128,2048]{2,1,0:T(8,128)(2,1)S(1)}, bf16[1,128,2048]{2,1,0:T(8,128)(2,1)}, u32[]{:S(2)}) %copy-start) | copy-done | bytes 524312
  1.7 0.0 copy-start.1
  1.7 1.0 %copy-done.1 = bf16[1,128,2048]{2,1,0:T(8,128)(2,1)S(1)} copy-done((bf16[1,128,2048]{2,1,0:T(8,128)(2,1)S(1)}, bf16[1,128,2048]{2,1,0:T(8,128)(2,1)}, u32[]{:S(2)}) %copy-start.1) | copy-done | bytes 524312
  2.7 0.8 copy-done.2
  3.5 0.4 shard_map.50
  3.9 40.7 %all_to_all.15.blocks_ref = bf16[32,136,128]{2,1,0:T(8,128)(2,1)S(1)} all-to-all(bf16[32,136,128]{2,1,0:T(8,128)(2,1)S(1)} %shard_map.50), channel_id=1, replica_groups=mesh['x'=4,'zh'=4,'y'=8,'w'=4] {'y','w'}, dimensions={0} | all-to-all | bytes 2228224 | tf_op jit(solution)/shard_map/all_to_all | solution.py:209
  44.6 4.8 %shard_map.52 = f32[32,4,128]{2,1,0:T(4,128)} custom-call(bf16[32,136,128]{2,1,0:T(8,128)(2,1)S(1)} %all_to_all.15.blocks_ref), custom_call_target="tpu_custom_call" | custom-call | flops 2147483648 | bytes 1048576 | tf_op jit(solution)/shard_map/pallas_call | solution.py:21
  49.4 5.4 %all-to-all-start.1 = ((f32[32,4,128]{2,1,0:T(4,128)}), f32[32,4,128]{2,1,0:T(4,128)S(1)}, u32[]{:S(2)}, u32[]{:S(2)}) async-start(f32[32,4,128]{2,1,0:T(4,128)} %shard_map.52), calls=%async_computation.1 | async-start | bytes 131072 | tf_op jit(solution)/shard_map/all_to_all | solution.py:222
  54.8 4.4 %shard_map.51 = bf16[32,64,128]{2,1,0:T(8,128)(2,1)} custom-call(bf16[32,136,128]{2,1,0:T(8,128)(2,1)S(1)} %all_to_all.15.blocks_ref), custom_call_target="tpu_custom_call" | custom-call | flops 2147483648 | bytes 1048576 | tf_op jit(solution)/shard_map/pallas_call | solution.py:21
  59.2 4.4 %all-to-all-done.1.came_ref = f32[32,4,128]{2,1,0:T(4,128)S(1)} async-done(((f32[32,4,128]{2,1,0:T(4,128)}), f32[32,4,128]{2,1,0:T(4,128)S(1)}, u32[]{:S(2)}, u32[]{:S(2)}) %all-to-all-start.1) | async-done | bytes 65568 | tf_op jit(solution)/shard_map/all_to_all | solution.py:222
  63.6 5.5 %all-to-all-start.2 = ((bf16[32,64,128]{2,1,0:T(8,128)(2,1)}), bf16[32,64,128]{2,1,0:T(8,128)(2,1)S(1)}, u32[]{:S(2)}, u32[]{:S(2)}) async-start(bf16[32,64,128]{2,1,0:T(8,128)(2,1)} %shard_map.51), calls=%async_computation.2 | async-start | bytes 1048576 | tf_op jit(solution)/shard_map/all_to_all | solution.py:236
  69.1 0.1 shard_map.54
  69.2 6.0 %collective-permute-start = (f32[8,128]{1,0:T(8,128)S(1)}, f32[8,128]{1,0:T(8,128)S(1)}, u32[]{:S(2)}, u32[]{:S(2)}) collective-permute-start(f32[8,128]{1,0:T(8,128)S(1)} %get-tuple-element.10), channel_id=1, source_target_pairs={{0,0},{1,32},{2,64},{3,96},{32,1},{33,33},{34,65},{35,97},{64,2},{... | collective-permute-start | bytes 12296 | tf_op jit(solution)/shard_map/ppermute | solution.py:248
  75.2 1.9 %collective-permute-start.1 = (f32[8,128]{1,0:T(8,128)S(1)}, f32[8,128]{1,0:T(8,128)S(1)}, u32[]{:S(2)}, u32[]{:S(2)}) collective-permute-start(f32[8,128]{1,0:T(8,128)S(1)} %get-tuple-element.11), channel_id=1, source_target_pairs={{0,1},{1,33},{2,65},{3,97},{32,2},{33,34},{34,66},{35,98},{64,3},{... | collective-permute-start | bytes 12296 | tf_op jit(solution)/shard_map/ppermute | solution.py:248
  77.2 6.3 %collective-permute-start.2 = (f32[8,128]{1,0:T(8,128)S(1)}, f32[8,128]{1,0:T(8,128)S(1)}, u32[]{:S(2)}, u32[]{:S(2)}) collective-permute-start(f32[8,128]{1,0:T(8,128)S(1)} %get-tuple-element.12), channel_id=1, source_target_pairs={{0,2},{1,34},{2,66},{3,98},{32,3},{33,35},{34,67},{35,99},{64,0},{... | collective-permute-start | bytes 12296 | tf_op jit(solution)/shard_map/ppermute | solution.py:248
  83.4 5.0 %collective-permute-start.3 = (f32[8,128]{1,0:T(8,128)S(1)}, f32[8,128]{1,0:T(8,128)S(1)}, u32[]{:S(2)}, u32[]{:S(2)}) collective-permute-start(f32[8,128]{1,0:T(8,128)S(1)} %get-tuple-element.13), channel_id=1, source_target_pairs={{0,3},{1,35},{2,67},{3,99},{32,0},{33,32},{34,64},{35,96},{64,1},{... | collective-permute-start | bytes 12296 | tf_op jit(solution)/shard_map/ppermute | solution.py:248
  88.4 0.0 collective-permute-done.refs_0_
  88.5 0.0 collective-permute-done.1.refs_1_
  88.5 0.0 collective-permute-done.2.refs_2_
  88.5 3.8 %collective-permute-done.3.refs_3_ = f32[8,128]{1,0:T(8,128)S(1)} collective-permute-done((f32[8,128]{1,0:T(8,128)S(1)}, f32[8,128]{1,0:T(8,128)S(1)}, u32[]{:S(2)}, u32[]{:S(2)}) %collective-permute-start.3) | collective-permute-done | bytes 4128 | tf_op jit(solution)/shard_map/ppermute | solution.py:248
  92.3 0.6 shard_map.55
  92.9 0.0 all-to-all-done.2.blocks_ref
  92.9 1.0 %shard_map.53 = bf16[128,2048]{1,0:T(8,128)(2,1)} custom-call(bf16[32,64,128]{2,1,0:T(8,128)(2,1)S(1)} %all-to-all-done.2.blocks_ref), custom_call_target="tpu_custom_call" | custom-call | flops 1048576 | bytes 1048576 | tf_op jit(solution)/shard_map/pallas_call | solution.py:21
  (1 shorter events, 0.0 us)
Async XLA Ops:
  0.6 1.0 %copy-start = (bf16[1,128,2048]{2,1,0:T(8,128)(2,1)S(1)}, bf16[1,128,2048]{2,1,0:T(8,128)(2,1)}, u32[]{:S(2)}) copy-start(bf16[1,128,2048]{2,1,0:T(8,128)(2,1)} %param.3) | copy-start | bytes 1572868
  1.7 1.0 %copy-start.1 = (bf16[1,128,2048]{2,1,0:T(8,128)(2,1)S(1)}, bf16[1,128,2048]{2,1,0:T(8,128)(2,1)}, u32[]{:S(2)}) copy-start(bf16[1,128,2048]{2,1,0:T(8,128)(2,1)} %param.4) | copy-start | bytes 1572868
  2.7 0.8 copy-start.2
  49.4 14.2 %all-to-all-start.1 = ((f32[32,4,128]{2,1,0:T(4,128)}), f32[32,4,128]{2,1,0:T(4,128)S(1)}, u32[]{:S(2)}, u32[]{:S(2)}) async-start(f32[32,4,128]{2,1,0:T(4,128)} %shard_map.52), calls=%async_computation.1 | async-start | bytes 131072 | tf_op jit(solution)/shard_map/all_to_all | solution.py:222
  63.6 29.3 %all-to-all-start.2 = ((bf16[32,64,128]{2,1,0:T(8,128)(2,1)}), bf16[32,64,128]{2,1,0:T(8,128)(2,1)S(1)}, u32[]{:S(2)}, u32[]{:S(2)}) async-start(bf16[32,64,128]{2,1,0:T(8,128)(2,1)} %shard_map.51), calls=%async_computation.2 | async-start | bytes 1048576 | tf_op jit(solution)/shard_map/all_to_all | solution.py:236
  69.2 19.3 %collective-permute-start = (f32[8,128]{1,0:T(8,128)S(1)}, f32[8,128]{1,0:T(8,128)S(1)}, u32[]{:S(2)}, u32[]{:S(2)}) collective-permute-start(f32[8,128]{1,0:T(8,128)S(1)} %get-tuple-element.10), channel_id=1, source_target_pairs={{0,0},{1,32},{2,64},{3,96},{32,1},{33,33},{34,65},{35,97},{64,2},{... | collective-permute-start | bytes 12296 | tf_op jit(solution)/shard_map/ppermute | solution.py:248
  75.2 13.2 %collective-permute-start.1 = (f32[8,128]{1,0:T(8,128)S(1)}, f32[8,128]{1,0:T(8,128)S(1)}, u32[]{:S(2)}, u32[]{:S(2)}) collective-permute-start(f32[8,128]{1,0:T(8,128)S(1)} %get-tuple-element.11), channel_id=1, source_target_pairs={{0,1},{1,33},{2,65},{3,97},{32,2},{33,34},{34,66},{35,98},{64,3},{... | collective-permute-start | bytes 12296 | tf_op jit(solution)/shard_map/ppermute | solution.py:248
  77.2 11.3 %collective-permute-start.2 = (f32[8,128]{1,0:T(8,128)S(1)}, f32[8,128]{1,0:T(8,128)S(1)}, u32[]{:S(2)}, u32[]{:S(2)}) collective-permute-start(f32[8,128]{1,0:T(8,128)S(1)} %get-tuple-element.12), channel_id=1, source_target_pairs={{0,2},{1,34},{2,66},{3,98},{32,3},{33,35},{34,67},{35,99},{64,0},{... | collective-permute-start | bytes 12296 | tf_op jit(solution)/shard_map/ppermute | solution.py:248
  83.4 8.9 %collective-permute-start.3 = (f32[8,128]{1,0:T(8,128)S(1)}, f32[8,128]{1,0:T(8,128)S(1)}, u32[]{:S(2)}, u32[]{:S(2)}) collective-permute-start(f32[8,128]{1,0:T(8,128)S(1)} %get-tuple-element.13), channel_id=1, source_target_pairs={{0,3},{1,35},{2,67},{3,99},{32,0},{33,32},{34,64},{35,96},{64,1},{... | collective-permute-start | bytes 12296 | tf_op jit(solution)/shard_map/ppermute | solution.py:248

commit v3 on v2

v3 whole, which is shorter than its diff:
```python
import math

import jax
import jax.numpy as jnp
from jax import lax
from jax.experimental import pallas as pl
from jax.experimental.pallas import tpu as pltpu
from jax.sharding import Mesh, PartitionSpec as P

GROUP = 16
LANES = 128
SPAN = 2 * LANES
SIDE = 4
MIB = 1024 * 1024
PACK_VMEM = 56 * MIB


def call(kernel, out_shape, *operands, scratch=(), flops=2**20, vmem=2 * MIB, space=pltpu.VMEM):
    whole = pl.BlockSpec(memory_space=space)
    several = isinstance(out_shape, (list, tuple))
    return pl.pallas_call(
        kernel,
        out_shape=out_shape,
        in_specs=[whole] * len(operands),
        out_specs=[whole] * len(out_shape) if several else whole,
        scratch_shapes=list(scratch),
        compiler_params=pltpu.CompilerParams(vmem_limit_bytes=vmem),
        cost_estimate=pl.CostEstimate(flops=flops, bytes_accessed=2**20, transcendentals=0),
    )(*operands)


def pack_kernel(
    saved_hbm, grad_hbm, filt_hbm, out_hbm, saved_ref, grad_ref, filt_ref, out_ref, lines_ref, sems
):
    places, groups = LANES // GROUP, SIDE
    channels = groups * GROUP
    width = SIDE * LANES
    filt_copy = pltpu.make_async_copy(filt_hbm, filt_ref, sems.at[0])
    filt_copy.start()
    copies = []
    for slot in range(groups):
        cols = pl.ds(slot * width, width)
        for kind, (source, target) in enumerate(((grad_hbm, grad_ref), (saved_hbm, saved_ref))):
            copy = pltpu.make_async_copy(
                source.at[:, cols], target.at[:, cols], sems.at[1 + 2 * slot + kind]
            )
            copy.start()
            copies.append(copy)
    filt_copy.wait()
    lines_ref[...] = filt_ref[...].astype(jnp.float32).T
    empty = jnp.zeros((out_ref.shape[2] - 2 * channels - groups, LANES), jnp.float32)
    for place in range(places):
        for inner in range(SIDE):
            first = inner * places + place
            mine = lines_ref[pl.ds(first, groups, stride=SIDE * places), :]
            block = jnp.concatenate([mine, empty], axis=0)
            out_ref[place, inner, 2 * channels :, :] = block.astype(jnp.bfloat16)
    for copy in copies:
        copy.wait()
    outs = []
    for inner in range(SIDE):
        for slot in range(groups):
            tile = slot * SIDE + inner
            cols = slice(tile * LANES, (tile + 1) * LANES)
            grad_rows = grad_ref[:, cols].T
            saved_rows = saved_ref[:, cols].T
            row = slot * GROUP
            for place in range(places):
                mine = slice(place * GROUP, (place + 1) * GROUP)
                out_ref[place, inner, row : row + GROUP, :] = grad_rows[mine, :]
                out_ref[place, inner, channels + row : channels + row + GROUP, :] = saved_rows[
                    mine, :
                ]
        copy = pltpu.make_async_copy(
            out_ref.at[:, inner], out_hbm.at[:, inner], sems.at[1 + 2 * groups + inner]
        )
        copy.start()
        outs.append(copy)
    for copy in outs:
        copy.wait()


def unpack_kernel(blocks_ref, out_ref):
    places = LANES // GROUP
    for tile in range(out_ref.shape[1] // LANES):
        slot, inner = tile // SIDE, tile % SIDE
        row = slot * GROUP
        rows = [
            blocks_ref[place * SIDE + inner, row : row + GROUP, :] for place in range(places)
        ]
        out_ref[:, tile * LANES : (tile + 1) * LANES] = jnp.concatenate(rows, axis=0).T


def widen_blocks(blocks_ref, first, wide_ref):
    for part in range(blocks_ref.shape[0]):
        row = (part // 2) * GROUP
        lane = (part % 2) * LANES
        wide_ref[row : row + GROUP, lane : lane + LANES] = blocks_ref[
            part, pl.ds(first, GROUP), :
        ]


def input_kernel(blocks_ref, out_ref, line_ref, wide_ref, toep_ref):
    parts, channels, _ = out_ref.shape
    groups = channels // GROUP
    half = parts // 2
    rows = half * GROUP
    wide_ref[rows:, :] = jnp.zeros_like(wide_ref[rows:, :])
    line_ref[...] = jnp.zeros_like(line_ref)
    for part in range(parts):
        start = (part + 1) * LANES
        line_ref[:, start : start + LANES] = blocks_ref[part, 2 * channels :, :][
            : line_ref.shape[0]
        ].astype(jnp.float32)

    def per_group(group, carry):
        first = pl.multiple_of(group * GROUP, GROUP)
        widen_blocks(blocks_ref, first, wide_ref)
        line = line_ref[pl.ds(group, 1), :]
        spread = jnp.broadcast_to(line, (LANES, line.shape[1]))
        toep_ref[...] = pltpu.roll(spread, 0, 1, stride=1, stride_axis=0).astype(jnp.bfloat16)
        total = jnp.zeros((rows, SPAN), jnp.float32)
        for lag in range(half):
            start = lag * SPAN
            taps = jnp.concatenate(
                [
                    toep_ref[:, start + LANES : start + LANES + SPAN],
                    toep_ref[:, start : start + SPAN],
                ],
                axis=0,
            )
            total = total + lax.dot_general(
                wide_ref[lag * GROUP : lag * GROUP + rows, :],
                taps,
                (((1,), (1,)), ((), ())),
                preferred_element_type=jnp.float32,
            )
        done = total.astype(jnp.bfloat16)
        for part in range(parts):
            row = (part // 2) * GROUP
            lane = (part % 2) * LANES
            out_ref[part, pl.ds(first, GROUP), :] = done[
                row : row + GROUP, lane : lane + LANES
            ]
        return carry

    lax.fori_loop(0, groups, per_group, 0)


def filter_kernel(blocks_ref, out_ref, tall_ref, saved_ref, product_ref):
    parts = blocks_ref.shape[0]
    rows = parts * GROUP
    groups = SIDE
    channels = groups * GROUP
    row_ids = lax.broadcasted_iota(jnp.int32, (LANES, LANES), 0)
    col_ids = lax.broadcasted_iota(jnp.int32, (LANES, LANES), 1)
    flip = jnp.where(row_ids + col_ids == LANES - 1, 1.0, 0.0).astype(jnp.bfloat16)
    empty = jnp.zeros((LANES, LANES), jnp.float32)
    product_ref[:, :LANES] = empty
    product_ref[:, (parts + 1) * LANES :] = empty
    tall_ref[rows - GROUP :, LANES:] = jnp.zeros((GROUP, LANES), jnp.bfloat16)
    for group in range(groups):
        first = group * GROUP
        for part in range(parts):
            mine = blocks_ref[part, first : first + GROUP, :]
            here = slice(part * GROUP, (part + 1) * GROUP)
            tall_ref[here, :LANES] = mine
            if part > 0:
                tall_ref[(part - 1) * GROUP : part * GROUP, LANES:] = mine
            saved_ref[here, :] = blocks_ref[part, channels + first : channels + first + GROUP, :]
        flipped = lax.dot_general(
            flip, saved_ref[...], (((1,), (1,)), ((), ())), preferred_element_type=jnp.float32
        ).astype(jnp.bfloat16)
        for pair in range(parts // 2):
            start = 2 * pair * GROUP
            depth = rows - start
            product_ref[:, LANES + pair * SPAN : LANES + (pair + 1) * SPAN] = jnp.dot(
                flipped[:, :depth], tall_ref[start:, :], preferred_element_type=jnp.float32
            )
        turned = pltpu.roll(product_ref[...], 1, 1, stride=1, stride_axis=0)
        line = jnp.sum(turned, axis=0, keepdims=True)
        for part in range(parts):
            start = SPAN + part * LANES
            out_ref[group * parts + part] = line[:, start : start + LANES]


def split_kernel(came_ref, keep_ref, send_ref, total_ref):
    parts = came_ref.shape[0] // SIDE
    places = parts // SIDE
    total = came_ref[:parts]
    for step in range(1, SIDE):
        total = total + came_ref[step * parts : (step + 1) * parts]
    total_ref[...] = total.reshape(parts, LANES)
    half = lax.axis_index("zh") // 2
    for low in range(2):
        here = slice(low * places, (low + 1) * places)
        mine, other = 2 * half + low, 2 * (1 - half) + low
        keep_ref[here, :] = total_ref[pl.ds(mine, places, stride=SIDE), :]
        send_ref[here, :] = total_ref[pl.ds(other, places, stride=SIDE), :]


def halve_kernel(kept_ref, came_ref, keep_ref, send_ref, total_ref):
    places = keep_ref.shape[0]
    total_ref[...] = kept_ref[...] + came_ref[...]
    half = lax.axis_index("zh") % 2
    keep_ref[...] = total_ref[pl.ds(pl.multiple_of(half * places, places), places), :]
    send_ref[...] = total_ref[pl.ds(pl.multiple_of((1 - half) * places, places), places), :]


def last_kernel(scale, kept_ref, came_ref, out_ref):
    out_ref[...] = (kept_ref[...] + came_ref[...]) * scale


def on_device(u_saved, grad_out, filters):
    tokens, width = u_saved.shape[1:]
    parts = lax.axis_size(("y", "w"))
    seqs = lax.axis_size(("x", "zh"))
    places = lax.axis_size("y")
    channels = width // parts
    groups = channels // GROUP
    length = parts * LANES
    bf16, f32 = jnp.bfloat16, jnp.float32
    half_rows = parts // 2 * GROUP

    rows = 2 * channels + 8
    packed = call(
        pack_kernel,
        jax.ShapeDtypeStruct((places, SIDE, rows, LANES), bf16),
        u_saved[0],
        grad_out[0],
        filters,
        scratch=[
            pltpu.VMEM((tokens, width), bf16),
            pltpu.VMEM((tokens, width), bf16),
            pltpu.VMEM(filters.shape, bf16),
            pltpu.VMEM((places, SIDE, rows, LANES), bf16),
            pltpu.VMEM((LANES, LANES), f32),
            pltpu.SemaphoreType.DMA((1 + 2 * groups + SIDE,)),
        ],
        vmem=PACK_VMEM,
        space=pl.ANY,
    ).reshape(parts, rows, LANES)
    blocks = lax.all_to_all(packed, ("y", "w"), split_axis=0, concat_axis=0, tiled=True)
    lags = call(
        filter_kernel,
        jax.ShapeDtypeStruct((SIDE * parts, 1, LANES), f32),
        blocks,
        scratch=[
            pltpu.VMEM((2 * half_rows, SPAN), bf16),
            pltpu.VMEM((2 * half_rows, LANES), bf16),
            pltpu.VMEM((LANES, length + SPAN), f32),
        ],
        flops=2**31,
        vmem=20 * MIB,
    )
    lags_came = lax.all_to_all(lags, ("x", "y", "w"), split_axis=0, concat_axis=0, tiled=True)
    input_blocks = call(
        input_kernel,
        jax.ShapeDtypeStruct((parts, channels, LANES), bf16),
        blocks,
        scratch=[
            pltpu.VMEM((groups, length + SPAN), f32),
            pltpu.VMEM((2 * half_rows, SPAN), bf16),
            pltpu.VMEM((LANES, length + SPAN), bf16),
        ],
        flops=2**31,
        vmem=20 * MIB,
    )
    input_blocks, lags_came = lax.optimization_barrier((input_blocks, lags_came))
    returned = lax.all_to_all(input_blocks, ("y", "w"), split_axis=0, concat_axis=0, tiled=True)
    halves = [jax.ShapeDtypeStruct((2 * places, LANES), f32)] * 2
    whole_places = jax.ShapeDtypeStruct((places, LANES), f32)
    kept, sent = call(split_kernel, halves, lags_came, scratch=[pltpu.VMEM((parts, LANES), f32)])
    far = lax.ppermute(sent, "zh", [(side, side ^ 2) for side in range(SIDE)])
    kept, sent = call(
        halve_kernel,
        [whole_places] * 2,
        kept,
        far,
        scratch=[pltpu.VMEM((2 * places, LANES), f32)],
    )
    near = lax.ppermute(sent, "zh", [(side, side ^ 1) for side in range(SIDE)])
    input_grad = call(
        unpack_kernel, jax.ShapeDtypeStruct((tokens, width), bf16), returned, vmem=4 * MIB
    )
    scale = 1.0 / math.sqrt(GROUP * seqs * length)
    input_grad, near = lax.optimization_barrier((input_grad, near))
    filter_part = call(lambda *refs: last_kernel(scale, *refs), whole_places, kept, near)
    return (input_grad[None], filter_part.T)


def solution(mesh):
    cut = Mesh(mesh.devices.reshape(SIDE, SIDE, -1, SIDE), ("x", "zh", "y", "w"))
    seq, token = ("x", "zh"), ("y", "w")
    in_specs = (P(seq, token, None), P(seq, token, None), P(token, None))
    out_specs = (P(seq, token, None), P(token, seq))
    return jax.shard_map(
        on_device, mesh=cut, in_specs=in_specs, out_specs=out_specs, check_vma=False
    )
```

time: 94.4 us -> 88.5 us (0.937)
  starting transfers between devices: 30.1 us -> 25.1 us
  local copies, waits for them, and re-layouts: 2.83 us -> 0 us
  waiting for transfers between devices: 8.24 us -> 9.34 us
    ppermute x4 -> x2, starting transfers between devices: 19.2 us -> 13.8 us  [the longest x1 9.72 us: on_device(): far = lax.ppermute(sent, 'zh', [(side, side ^ 2) for side in range(SIDE)])]
    unnamed x6 -> x0, local copies, waits for them, and re-layouts: 2.83 us -> none
    ppermute x4 -> x2, waiting for transfers between devices: 3.83 us -> 1.03 us  [the longest x1 1.03 us: on_device(): far = lax.ppermute(sent, 'zh', [(side, side ^ 2) for side in range(SIDE)])]
    all_to_all x1, waiting for transfers between devices: 0.01 us -> 2.17 us  [on_device(): lax.all_to_all(input_blocks, ('y', 'w'), split_axis=0, concat_axis=0, til...]
    all_to_all x1, starting transfers between devices: 5.36 us -> 7.13 us  [on_device(): lax.all_to_all(lags, ('x', 'y', 'w'), split_axis=0, concat_axis=0, tiled=...]
    all_to_all x1, waiting for transfers between devices: 4.41 us -> 6.14 us  [on_device(): lax.all_to_all(lags, ('x', 'y', 'w'), split_axis=0, concat_axis=0, tiled=...]
    all_to_all x1, starting transfers between devices: 5.47 us -> 4.17 us  [on_device(): lax.all_to_all(input_blocks, ('y', 'w'), split_axis=0, concat_axis=0, til...]
    pallas_call x6 -> x7, Pallas kernels: 11.3 us -> 12 us  [call(): pl.pallas_call(kernel, out_shape=out_shape, in_specs=[whole] * len(operan...]
  transfers between devices with their start and end apart: 6 -> 4, of which waited for: 2 -> 3; matrix products, arithmetic and copies ran while one was open for 0% -> 0% of each run, Pallas kernels for 5% -> 6%
where the time goes in v3:
time: 88.5 us; the launch traced here: 88.1 us
  blocking collectives  40.9 us (46%)
  starting transfers between devices  25.1 us (28%)
  Pallas kernels  12 us (14%)
  waiting for transfers between devices  9.34 us (11%)
    all_to_all x1, blocking collectives, on_device(): lax.all_to_all(packed, ('y', 'w'), split_axis=0, concat_axis=0, tiled=True)  40.9 us
    pallas_call x7, Pallas kernels, call(): pl.pallas_call(kernel, out_shape=out_shape, in_specs=[whole] * len(operan...  12 us
    ppermute x1, starting transfers between devices, on_device(): far = lax.ppermute(sent, 'zh', [(side, side ^ 2) for side in range(SIDE)])  9.72 us
    all_to_all x1, starting transfers between devices, on_device(): lax.all_to_all(lags, ('x', 'y', 'w'), split_axis=0, concat_axis=0, tiled=...  7.13 us
    all_to_all x1, waiting for transfers between devices, on_device(): lax.all_to_all(lags, ('x', 'y', 'w'), split_axis=0, concat_axis=0, tiled=...  6.14 us
    all_to_all x1, starting transfers between devices, on_device(): lax.all_to_all(input_blocks, ('y', 'w'), split_axis=0, concat_axis=0, til...  4.17 us
    ppermute x1, starting transfers between devices, on_device(): near = lax.ppermute(sent, 'zh', [(side, side ^ 1) for side in range(SIDE)])  4.08 us
    all_to_all x1, waiting for transfers between devices, on_device(): lax.all_to_all(input_blocks, ('y', 'w'), split_axis=0, concat_axis=0, til...  2.17 us
  transfers between devices with their start and end apart: 4, of which 3 were waited for; matrix products, arithmetic and copies ran while one was open for 0% of the time, Pallas kernels for 6%

profile of v3, /device:TPU:1, one launch (start us, length us, event | category | flops | bytes accessed | tf_op | source)
XLA Modules:
  0.0 88.1 jit_solution(906140802126392252)
XLA Ops:
  0.6 2.6 %shard_map.50 = bf16[8,4,136,128]{3,2,1,0:T(8,128)(2,1)} custom-call(bf16[128,2048]{1,0:T(8,128)(2,1)} %bitcast.7, bf16[128,2048]{1,0:T(8,128)(2,1)} %bitcast.8, bf16[128,128]{1,0:T(8,128)(2,1)} %filt_hbm.1), custom_call_target="tpu_custom_call" | custom-call | flops 1048576 | bytes 1048576 | tf_op jit(solution)/shard_map/pallas_call | solution.py:21
  3.2 40.9 %all_to_all.15.blocks_ref = bf16[32,136,128]{2,1,0:T(8,128)(2,1)S(1)} all-to-all(bf16[32,136,128]{2,1,0:T(8,128)(2,1)} %bitcast.5), channel_id=1, replica_groups=mesh['x'=4,'zh'=4,'y'=8,'w'=4] {'y','w'}, dimensions={0} | all-to-all | bytes 2228224 | tf_op jit(solution)/shard_map/all_to_all | solution.py:243
  44.1 3.4 %shard_map.52 = f32[128,1,128]{2,1,0:T(1,128)} custom-call(bf16[32,136,128]{2,1,0:T(8,128)(2,1)S(1)} %all_to_all.15.blocks_ref), custom_call_target="tpu_custom_call" | custom-call | flops 2147483648 | bytes 1048576 | tf_op jit(solution)/shard_map/pallas_call | solution.py:21
  47.5 7.1 %all-to-all-start.1 = ((f32[128,1,128]{2,1,0:T(1,128)}), f32[128,1,128]{2,1,0:T(1,128)S(1)}, u32[]{:S(2)}, u32[]{:S(2)}) async-start(f32[128,1,128]{2,1,0:T(1,128)} %shard_map.52), calls=%async_computation.1 | async-start | bytes 131072 | tf_op jit(solution)/shard_map/all_to_all | solution.py:256
  54.6 4.5 %shard_map.51 = bf16[32,64,128]{2,1,0:T(8,128)(2,1)} custom-call(bf16[32,136,128]{2,1,0:T(8,128)(2,1)S(1)} %all_to_all.15.blocks_ref), custom_call_target="tpu_custom_call" | custom-call | flops 2147483648 | bytes 1048576 | tf_op jit(solution)/shard_map/pallas_call | solution.py:21
  59.1 6.1 %all-to-all-done.1.came_ref = f32[128,1,128]{2,1,0:T(1,128)S(1)} async-done(((f32[128,1,128]{2,1,0:T(1,128)}), f32[128,1,128]{2,1,0:T(1,128)S(1)}, u32[]{:S(2)}, u32[]{:S(2)}) %all-to-all-start.1) | async-done | bytes 65568 | tf_op jit(solution)/shard_map/all_to_all | solution.py:256
  65.2 4.2 %all-to-all-start.2 = ((bf16[32,64,128]{2,1,0:T(8,128)(2,1)}), bf16[32,64,128]{2,1,0:T(8,128)(2,1)S(1)}, u32[]{:S(2)}, u32[]{:S(2)}) async-start(bf16[32,64,128]{2,1,0:T(8,128)(2,1)} %shard_map.51), calls=%async_computation.2 | async-start | bytes 1048576 | tf_op jit(solution)/shard_map/all_to_all | solution.py:270
  69.5 9.7 %collective-permute-start = (f32[16,128]{1,0:T(8,128)S(1)}, f32[16,128]{1,0:T(8,128)S(1)}, u32[]{:S(2)}, u32[]{:S(2)}) collective-permute-start(f32[16,128]{1,0:T(8,128)S(1)} %get-tuple-element.13), channel_id=1, source_target_pairs={{0,64},{32,96},{64,0},{96,32},{1,65},{33,97},{65,1},{97,33},{2,66}... | collective-permute-start | bytes 24584 | tf_op jit(solution)/shard_map/ppermute | solution.py:274
  79.2 1.0 %collective-permute-done.came_ref = f32[16,128]{1,0:T(8,128)S(1)} collective-permute-done((f32[16,128]{1,0:T(8,128)S(1)}, f32[16,128]{1,0:T(8,128)S(1)}, u32[]{:S(2)}, u32[]{:S(2)}) %collective-permute-start) | collective-permute-done | bytes 8224 | tf_op jit(solution)/shard_map/ppermute | solution.py:274
  80.2 4.1 %collective-permute-start.1 = (f32[8,128]{1,0:T(8,128)S(1)}, f32[8,128]{1,0:T(8,128)S(1)}, u32[]{:S(2)}, u32[]{:S(2)}) collective-permute-start(f32[8,128]{1,0:T(8,128)S(1)} %get-tuple-element.14), channel_id=1, source_target_pairs={{0,32},{32,0},{64,96},{96,64},{1,33},{33,1},{65,97},{97,65},{2,34}... | collective-permute-start | bytes 12296 | tf_op jit(solution)/shard_map/ppermute | solution.py:282
  84.3 2.2 %all-to-all-done.2.blocks_ref = bf16[32,64,128]{2,1,0:T(8,128)(2,1)S(1)} async-done(((bf16[32,64,128]{2,1,0:T(8,128)(2,1)}), bf16[32,64,128]{2,1,0:T(8,128)(2,1)S(1)}, u32[]{:S(2)}, u32[]{:S(2)}) %all-to-all-start.2) | async-done | bytes 524320 | tf_op jit(solution)/shard_map/all_to_all | solution.py:270
  86.5 1.0 %shard_map.53 = bf16[128,2048]{1,0:T(8,128)(2,1)} custom-call(bf16[32,64,128]{2,1,0:T(8,128)(2,1)S(1)} %all-to-all-done.2.blocks_ref), custom_call_target="tpu_custom_call" | custom-call | flops 1048576 | bytes 1048576 | tf_op jit(solution)/shard_map/pallas_call | solution.py:21
  87.5 0.0 collective-permute-done.1.refs_1_
  87.5 0.6 shard_map.56
  (2 shorter events, 0.1 us)
Async XLA Ops:
  47.5 17.7 %all-to-all-start.1 = ((f32[128,1,128]{2,1,0:T(1,128)}), f32[128,1,128]{2,1,0:T(1,128)S(1)}, u32[]{:S(2)}, u32[]{:S(2)}) async-start(f32[128,1,128]{2,1,0:T(1,128)} %shard_map.52), calls=%async_computation.1 | async-start | bytes 131072 | tf_op jit(solution)/shard_map/all_to_all | solution.py:256
  65.2 21.3 %all-to-all-start.2 = ((bf16[32,64,128]{2,1,0:T(8,128)(2,1)}), bf16[32,64,128]{2,1,0:T(8,128)(2,1)S(1)}, u32[]{:S(2)}, u32[]{:S(2)}) async-start(bf16[32,64,128]{2,1,0:T(8,128)(2,1)} %shard_map.51), calls=%async_computation.2 | async-start | bytes 1048576 | tf_op jit(solution)/shard_map/all_to_all | solution.py:270
  69.5 10.8 %collective-permute-start = (f32[16,128]{1,0:T(8,128)S(1)}, f32[16,128]{1,0:T(8,128)S(1)}, u32[]{:S(2)}, u32[]{:S(2)}) collective-permute-start(f32[16,128]{1,0:T(8,128)S(1)} %get-tuple-element.13), channel_id=1, source_target_pairs={{0,64},{32,96},{64,0},{96,32},{1,65},{33,97},{65,1},{97,33},{2,66}... | collective-permute-start | bytes 24584 | tf_op jit(solution)/shard_map/ppermute | solution.py:274
  80.2 7.2 %collective-permute-start.1 = (f32[8,128]{1,0:T(8,128)S(1)}, f32[8,128]{1,0:T(8,128)S(1)}, u32[]{:S(2)}, u32[]{:S(2)}) collective-permute-start(f32[8,128]{1,0:T(8,128)S(1)} %get-tuple-element.14), channel_id=1, source_target_pairs={{0,32},{32,0},{64,96},{96,64},{1,33},{33,1},{65,97},{97,65},{2,34}... | collective-permute-start | bytes 12296 | tf_op jit(solution)/shard_map/ppermute | solution.py:282

commit v4 on v3

--- a/solution.py
+++ b/solution.py
@@ -12,16 +12,16 @@
 SPAN = 2 * LANES
 SIDE = 4
 MIB = 1024 * 1024
-PACK_VMEM = 56 * MIB
 
 
 def call(kernel, out_shape, *operands, scratch=(), flops=2**20, vmem=2 * MIB, space=pltpu.VMEM):
-    whole = pl.BlockSpec(memory_space=space)
+    given = pl.BlockSpec(memory_space=space)
+    whole = pl.BlockSpec(memory_space=pltpu.VMEM)
     several = isinstance(out_shape, (list, tuple))
     return pl.pallas_call(
         kernel,
         out_shape=out_shape,
-        in_specs=[whole] * len(operands),
+        in_specs=[given] * len(operands),
         out_specs=[whole] * len(out_shape) if several else whole,
         scratch_shapes=list(scratch),
         compiler_params=pltpu.CompilerParams(vmem_limit_bytes=vmem),
@@ -30,22 +30,16 @@
 
 
 def pack_kernel(
-    saved_hbm, grad_hbm, filt_hbm, out_hbm, saved_ref, grad_ref, filt_ref, out_ref, lines_ref, sems
+    saved_hbm, grad_hbm, filt_hbm, out_ref, saved_ref, grad_ref, filt_ref, lines_ref, sems
 ):
     places, groups = LANES // GROUP, SIDE
     channels = groups * GROUP
-    width = SIDE * LANES
     filt_copy = pltpu.make_async_copy(filt_hbm, filt_ref, sems.at[0])
     filt_copy.start()
-    copies = []
-    for slot in range(groups):
-        cols = pl.ds(slot * width, width)
-        for kind, (source, target) in enumerate(((grad_hbm, grad_ref), (saved_hbm, saved_ref))):
-            copy = pltpu.make_async_copy(
-                source.at[:, cols], target.at[:, cols], sems.at[1 + 2 * slot + kind]
-            )
-            copy.start()
-            copies.append(copy)
+    grad_copy = pltpu.make_async_copy(grad_hbm, grad_ref, sems.at[1])
+    saved_copy = pltpu.make_async_copy(saved_hbm, saved_ref, sems.at[2])
+    grad_copy.start()
+    saved_copy.start()
     filt_copy.wait()
     lines_ref[...] = filt_ref[...].astype(jnp.float32).T
     empty = jnp.zeros((out_ref.shape[2] - 2 * channels - groups, LANES), jnp.float32)
@@ -55,40 +49,18 @@
             mine = lines_ref[pl.ds(first, groups, stride=SIDE * places), :]
             block = jnp.concatenate([mine, empty], axis=0)
             out_ref[place, inner, 2 * channels :, :] = block.astype(jnp.bfloat16)
-    for copy in copies:
-        copy.wait()
-    outs = []
-    for inner in range(SIDE):
-        for slot in range(groups):
-            tile = slot * SIDE + inner
-            cols = slice(tile * LANES, (tile + 1) * LANES)
-            grad_rows = grad_ref[:, cols].T
-            saved_rows = saved_ref[:, cols].T
-            row = slot * GROUP
-            for place in range(places):
-                mine = slice(place * GROUP, (place + 1) * GROUP)
-                out_ref[place, inner, row : row + GROUP, :] = grad_rows[mine, :]
-                out_ref[place, inner, channels + row : channels + row + GROUP, :] = saved_rows[
-                    mine, :
-                ]
-        copy = pltpu.make_async_copy(
-            out_ref.at[:, inner], out_hbm.at[:, inner], sems.at[1 + 2 * groups + inner]
-        )
-        copy.start()
-        outs.append(copy)
-    for copy in outs:
-        copy.wait()
-
-
-def unpack_kernel(blocks_ref, out_ref):
-    places = LANES // GROUP
-    for tile in range(out_ref.shape[1] // LANES):
+    grad_copy.wait()
+    saved_copy.wait()
+    for tile in range(groups * SIDE):
         slot, inner = tile // SIDE, tile % SIDE
+        cols = slice(tile * LANES, (tile + 1) * LANES)
+        grad_rows = grad_ref[:, cols].T
+        saved_rows = saved_ref[:, cols].T
         row = slot * GROUP
-        rows = [
-            blocks_ref[place * SIDE + inner, row : row + GROUP, :] for place in range(places)
-        ]
-        out_ref[:, tile * LANES : (tile + 1) * LANES] = jnp.concatenate(rows, axis=0).T
+        for place in range(places):
+            mine = slice(place * GROUP, (place + 1) * GROUP)
+            out_ref[place, inner, row : row + GROUP, :] = grad_rows[mine, :]
+            out_ref[place, inner, channels + row : channels + row + GROUP, :] = saved_rows[mine, :]
 
 
 def widen_blocks(blocks_ref, first, wide_ref):
@@ -96,55 +68,62 @@
         row = (part // 2) * GROUP
         lane = (part % 2) * LANES
         wide_ref[row : row + GROUP, lane : lane + LANES] = blocks_ref[
-            part, pl.ds(first, GROUP), :
+            part, first : first + GROUP, :
         ]
 
 
-def input_kernel(blocks_ref, out_ref, line_ref, wide_ref, toep_ref):
+def input_kernel(blocks_ref, out_ref, line_ref, wide_refs, toep_refs):
     parts, channels, _ = out_ref.shape
     groups = channels // GROUP
     half = parts // 2
     rows = half * GROUP
-    wide_ref[rows:, :] = jnp.zeros_like(wide_ref[rows:, :])
+    slots = wide_refs.shape[0]
+    for slot in range(slots):
+        wide_refs[slot, rows:, :] = jnp.zeros((rows, SPAN), jnp.bfloat16)
     line_ref[...] = jnp.zeros_like(line_ref)
     for part in range(parts):
         start = (part + 1) * LANES
-        line_ref[:, start : start + LANES] = blocks_ref[part, 2 * channels :, :][
-            : line_ref.shape[0]
-        ].astype(jnp.float32)
-
-    def per_group(group, carry):
-        first = pl.multiple_of(group * GROUP, GROUP)
-        widen_blocks(blocks_ref, first, wide_ref)
-        line = line_ref[pl.ds(group, 1), :]
+        line_ref[:, start : start + LANES] = blocks_ref[part, 2 * channels :, :][:groups].astype(
+            jnp.float32
+        )
+
+    def prepare(group):
+        slot = group % slots
+        widen_blocks(blocks_ref, group * GROUP, wide_refs.at[slot])
+        line = line_ref[group : group + 1, :]
         spread = jnp.broadcast_to(line, (LANES, line.shape[1]))
-        toep_ref[...] = pltpu.roll(spread, 0, 1, stride=1, stride_axis=0).astype(jnp.bfloat16)
+        toep_refs[slot] = pltpu.roll(spread, 0, 1, stride=1, stride_axis=0).astype(jnp.bfloat16)
+
+    def multiply(group):
+        slot = group % slots
         total = jnp.zeros((rows, SPAN), jnp.float32)
         for lag in range(half):
             start = lag * SPAN
             taps = jnp.concatenate(
                 [
-                    toep_ref[:, start + LANES : start + LANES + SPAN],
-                    toep_ref[:, start : start + SPAN],
+                    toep_refs[slot, :, start + LANES : start + LANES + SPAN],
+                    toep_refs[slot, :, start : start + SPAN],
                 ],
                 axis=0,
             )
             total = total + lax.dot_general(
-                wide_ref[lag * GROUP : lag * GROUP + rows, :],
+                wide_refs[slot, lag * GROUP : lag * GROUP + rows, :],
                 taps,
                 (((1,), (1,)), ((), ())),
                 preferred_element_type=jnp.float32,
             )
         done = total.astype(jnp.bfloat16)
+        first = group * GROUP
         for part in range(parts):
             row = (part // 2) * GROUP
             lane = (part % 2) * LANES
-            out_ref[part, pl.ds(first, GROUP), :] = done[
-                row : row + GROUP, lane : lane + LANES
-            ]
-        return carry
-
-    lax.fori_loop(0, groups, per_group, 0)
+            out_ref[part, first : first + GROUP, :] = done[row : row + GROUP, lane : lane + LANES]
+
+    prepare(0)
+    for group in range(groups):
+        if group + 1 < groups:
+            prepare(group + 1)
+        multiply(group)
 
 
 def filter_kernel(blocks_ref, out_ref, tall_ref, saved_ref, product_ref):
@@ -207,8 +186,16 @@
     send_ref[...] = total_ref[pl.ds(pl.multiple_of((1 - half) * places, places), places), :]
 
 
-def last_kernel(scale, kept_ref, came_ref, out_ref):
-    out_ref[...] = (kept_ref[...] + came_ref[...]) * scale
+def last_kernel(scale, blocks_ref, kept_ref, came_ref, input_ref, filter_ref):
+    filter_ref[...] = (kept_ref[...] + came_ref[...]) * scale
+    places = LANES // GROUP
+    for tile in range(input_ref.shape[1] // LANES):
+        slot, inner = tile // SIDE, tile % SIDE
+        row = slot * GROUP
+        rows = [
+            blocks_ref[place * SIDE + inner, row : row + GROUP, :] for place in range(places)
+        ]
+        input_ref[:, tile * LANES : (tile + 1) * LANES] = jnp.concatenate(rows, axis=0).T
 
 
 def on_device(u_saved, grad_out, filters):
@@ -226,19 +213,19 @@
     packed = call(
         pack_kernel,
         jax.ShapeDtypeStruct((places, SIDE, rows, LANES), bf16),
-        u_saved[0],
-        grad_out[0],
-        filters,
+        *(
+            pltpu.with_memory_space_constraint(array, pltpu.HBM)
+            for array in (u_saved[0], grad_out[0], filters)
+        ),
         scratch=[
             pltpu.VMEM((tokens, width), bf16),
             pltpu.VMEM((tokens, width), bf16),
             pltpu.VMEM(filters.shape, bf16),
-            pltpu.VMEM((places, SIDE, rows, LANES), bf16),
             pltpu.VMEM((LANES, LANES), f32),
-            pltpu.SemaphoreType.DMA((1 + 2 * groups + SIDE,)),
+            pltpu.SemaphoreType.DMA((3,)),
         ],
-        vmem=PACK_VMEM,
-        space=pl.ANY,
+        vmem=8 * MIB,
+        space=pltpu.HBM,
     ).reshape(parts, rows, LANES)
     blocks = lax.all_to_all(packed, ("y", "w"), split_axis=0, concat_axis=0, tiled=True)
     lags = call(
@@ -260,8 +247,8 @@
         blocks,
         scratch=[
             pltpu.VMEM((groups, length + SPAN), f32),
-            pltpu.VMEM((2 * half_rows, SPAN), bf16),
-            pltpu.VMEM((LANES, length + SPAN), bf16),
+            pltpu.VMEM((2, 2 * half_rows, SPAN), bf16),
+            pltpu.VMEM((2, LANES, length + SPAN), bf16),
         ],
         flops=2**31,
         vmem=20 * MIB,
@@ -280,12 +267,15 @@
         scratch=[pltpu.VMEM((2 * places, LANES), f32)],
     )
     near = lax.ppermute(sent, "zh", [(side, side ^ 1) for side in range(SIDE)])
-    input_grad = call(
-        unpack_kernel, jax.ShapeDtypeStruct((tokens, width), bf16), returned, vmem=4 * MIB
-    )
     scale = 1.0 / math.sqrt(GROUP * seqs * length)
-    input_grad, near = lax.optimization_barrier((input_grad, near))
-    filter_part = call(lambda *refs: last_kernel(scale, *refs), whole_places, kept, near)
+    input_grad, filter_part = call(
+        lambda *refs: last_kernel(scale, *refs),
+        [jax.ShapeDtypeStruct((tokens, width), bf16), whole_places],
+        returned,
+        kept,
+        near,
+        vmem=4 * MIB,
+    )
     return (input_grad[None], filter_part.T)
 
 

time: 88.5 us -> 86.7 us (0.980)
  Pallas kernels: 12 us -> 9.38 us
  waiting for transfers between devices: 9.34 us -> 10.4 us
    pallas_call x7 -> x6, Pallas kernels: 12 us -> 9.38 us  [call(): pl.pallas_call(kernel, out_shape=out_shape, in_specs=[given] * len(operan...]
    all_to_all x1, waiting for transfers between devices: 2.17 us -> 0.84 us  [on_device(): lax.all_to_all(input_blocks, ('y', 'w'), split_axis=0, concat_axis=0, til...]
    ppermute x1, waiting for transfers between devices: 0.01 us -> 1.32 us  [on_device(): near = lax.ppermute(sent, 'zh', [(side, side ^ 1) for side in range(SIDE)])]
    all_to_all x1, waiting for transfers between devices: 6.14 us -> 7.19 us  [on_device(): lax.all_to_all(lags, ('x', 'y', 'w'), split_axis=0, concat_axis=0, tiled=...]
  transfers between devices with their start and end apart: 4 -> 4, of which waited for: 3 -> 4; matrix products, arithmetic and copies ran while one was open for 0% -> 0% of each run, Pallas kernels for 6% -> 4%
where the time goes in v4:
time: 86.7 us; the launch traced here: 86.3 us
  blocking collectives  40.7 us (47%)
  starting transfers between devices  25.1 us (29%)
  waiting for transfers between devices  10.4 us (12%)
  Pallas kernels  9.38 us (11%)
    all_to_all x1, blocking collectives, on_device(): lax.all_to_all(packed, ('y', 'w'), split_axis=0, concat_axis=0, tiled=True)  40.7 us
    ppermute x1, starting transfers between devices, on_device(): far = lax.ppermute(sent, 'zh', [(side, side ^ 2) for side in range(SIDE)])  9.73 us
    pallas_call x6, Pallas kernels, call(): pl.pallas_call(kernel, out_shape=out_shape, in_specs=[given] * len(operan...  9.38 us
    all_to_all x1, waiting for transfers between devices, on_device(): lax.all_to_all(lags, ('x', 'y', 'w'), split_axis=0, concat_axis=0, tiled=...  7.19 us
    all_to_all x1, starting transfers between devices, on_device(): lax.all_to_all(lags, ('x', 'y', 'w'), split_axis=0, concat_axis=0, tiled=...  7.11 us
    all_to_all x1, starting transfers between devices, on_device(): lax.all_to_all(input_blocks, ('y', 'w'), split_axis=0, concat_axis=0, til...  4.18 us
    ppermute x1, starting transfers between devices, on_device(): near = lax.ppermute(sent, 'zh', [(side, side ^ 1) for side in range(SIDE)])  4.09 us
  transfers between devices with their start and end apart: 4, of which 4 were waited for; matrix products, arithmetic and copies ran while one was open for 0% of the time, Pallas kernels for 4%

profile of v4, /device:TPU:1, one launch (start us, length us, event | category | flops | bytes accessed | tf_op | source)
XLA Modules:
  0.0 86.3 jit_solution(10902380993263430389)
XLA Ops:
  0.6 1.6 %shard_map.50 = bf16[8,4,136,128]{3,2,1,0:T(8,128)(2,1)S(1)} custom-call(bf16[128,2048]{1,0:T(8,128)(2,1)} %bitcast.6, bf16[128,2048]{1,0:T(8,128)(2,1)} %bitcast.7, bf16[128,128]{1,0:T(8,128)(2,1)} %filt_hbm.1), custom_call_target="tpu_custom_call" | custom-call | flops 1048576 | bytes 1048576 | tf_op jit(solution)/shard_map/pallas_call | solution.py:21
  2.2 40.7 %all_to_all.15.blocks_ref = bf16[32,136,128]{2,1,0:T(8,128)(2,1)S(1)} all-to-all(bf16[32,136,128]{2,1,0:T(8,128)(2,1)S(1)} %bitcast.5), channel_id=1, replica_groups=mesh['x'=4,'zh'=4,'y'=8,'w'=4] {'y','w'}, dimensions={0} | all-to-all | bytes 2228224 | tf_op jit(solution)/shard_map/all_to_all | solution.py:230
  42.9 3.4 %shard_map.52 = f32[128,1,128]{2,1,0:T(1,128)} custom-call(bf16[32,136,128]{2,1,0:T(8,128)(2,1)S(1)} %all_to_all.15.blocks_ref), custom_call_target="tpu_custom_call" | custom-call | flops 2147483648 | bytes 1048576 | tf_op jit(solution)/shard_map/pallas_call | solution.py:21
  46.3 7.1 %all-to-all-start.1 = ((f32[128,1,128]{2,1,0:T(1,128)}), f32[128,1,128]{2,1,0:T(1,128)S(1)}, u32[]{:S(2)}, u32[]{:S(2)}) async-start(f32[128,1,128]{2,1,0:T(1,128)} %shard_map.52), calls=%async_computation.1 | async-start | bytes 131072 | tf_op jit(solution)/shard_map/all_to_all | solution.py:243
  53.4 3.4 %shard_map.51 = bf16[32,64,128]{2,1,0:T(8,128)(2,1)} custom-call(bf16[32,136,128]{2,1,0:T(8,128)(2,1)S(1)} %all_to_all.15.blocks_ref), custom_call_target="tpu_custom_call" | custom-call | flops 2147483648 | bytes 1048576 | tf_op jit(solution)/shard_map/pallas_call | solution.py:21
  56.8 7.2 %all-to-all-done.1.came_ref = f32[128,1,128]{2,1,0:T(1,128)S(1)} async-done(((f32[128,1,128]{2,1,0:T(1,128)}), f32[128,1,128]{2,1,0:T(1,128)S(1)}, u32[]{:S(2)}, u32[]{:S(2)}) %all-to-all-start.1) | async-done | bytes 65568 | tf_op jit(solution)/shard_map/all_to_all | solution.py:243
  64.0 4.2 %all-to-all-start.2 = ((bf16[32,64,128]{2,1,0:T(8,128)(2,1)}), bf16[32,64,128]{2,1,0:T(8,128)(2,1)S(1)}, u32[]{:S(2)}, u32[]{:S(2)}) async-start(bf16[32,64,128]{2,1,0:T(8,128)(2,1)} %shard_map.51), calls=%async_computation.2 | async-start | bytes 1048576 | tf_op jit(solution)/shard_map/all_to_all | solution.py:257
  68.2 9.7 %collective-permute-start = (f32[16,128]{1,0:T(8,128)S(1)}, f32[16,128]{1,0:T(8,128)S(1)}, u32[]{:S(2)}, u32[]{:S(2)}) collective-permute-start(f32[16,128]{1,0:T(8,128)S(1)} %get-tuple-element.13), channel_id=1, source_target_pairs={{0,64},{32,96},{64,0},{96,32},{1,65},{33,97},{65,1},{97,33},{2,66}... | collective-permute-start | bytes 24584 | tf_op jit(solution)/shard_map/ppermute | solution.py:261
  78.0 1.0 %collective-permute-done.came_ref = f32[16,128]{1,0:T(8,128)S(1)} collective-permute-done((f32[16,128]{1,0:T(8,128)S(1)}, f32[16,128]{1,0:T(8,128)S(1)}, u32[]{:S(2)}, u32[]{:S(2)}) %collective-permute-start) | collective-permute-done | bytes 8224 | tf_op jit(solution)/shard_map/ppermute | solution.py:261
  79.0 4.1 %collective-permute-start.1 = (f32[8,128]{1,0:T(8,128)S(1)}, f32[8,128]{1,0:T(8,128)S(1)}, u32[]{:S(2)}, u32[]{:S(2)}) collective-permute-start(f32[8,128]{1,0:T(8,128)S(1)} %get-tuple-element.15), channel_id=1, source_target_pairs={{0,32},{32,0},{64,96},{96,64},{1,33},{33,1},{65,97},{97,65},{2,34}... | collective-permute-start | bytes 12296 | tf_op jit(solution)/shard_map/ppermute | solution.py:269
  83.1 1.3 %collective-permute-done.1.refs_2_ = f32[8,128]{1,0:T(8,128)S(1)} collective-permute-done((f32[8,128]{1,0:T(8,128)S(1)}, f32[8,128]{1,0:T(8,128)S(1)}, u32[]{:S(2)}, u32[]{:S(2)}) %collective-permute-start.1) | collective-permute-done | bytes 4128 | tf_op jit(solution)/shard_map/ppermute | solution.py:269
  84.4 0.8 all-to-all-done.2.refs_0_
  85.3 1.0 %shard_map.55 = (bf16[128,2048]{1,0:T(8,128)(2,1)}, f32[8,128]{1,0:T(8,128)}) custom-call(bf16[32,64,128]{2,1,0:T(8,128)(2,1)S(1)} %all-to-all-done.2.refs_0_, f32[8,128]{1,0:T(8,128)S(1)} %get-tuple-element.14.refs_1_, f32[8,128]{1,0:T(8,128)S(1)} %collective-permute-done.1.refs_2_), custom_call_target="tpu_custom_call" | custom-call | flops 1048576 | bytes 1048576 | tf_op jit(solution)/shard_map/pallas_call | solution.py:21
  (2 shorter events, 0.1 us)
Async XLA Ops:
  46.3 17.7 %all-to-all-start.1 = ((f32[128,1,128]{2,1,0:T(1,128)}), f32[128,1,128]{2,1,0:T(1,128)S(1)}, u32[]{:S(2)}, u32[]{:S(2)}) async-start(f32[128,1,128]{2,1,0:T(1,128)} %shard_map.52), calls=%async_computation.1 | async-start | bytes 131072 | tf_op jit(solution)/shard_map/all_to_all | solution.py:243
  64.0 21.3 %all-to-all-start.2 = ((bf16[32,64,128]{2,1,0:T(8,128)(2,1)}), bf16[32,64,128]{2,1,0:T(8,128)(2,1)S(1)}, u32[]{:S(2)}, u32[]{:S(2)}) async-start(bf16[32,64,128]{2,1,0:T(8,128)(2,1)} %shard_map.51), calls=%async_computation.2 | async-start | bytes 1048576 | tf_op jit(solution)/shard_map/all_to_all | solution.py:257
  68.2 10.8 %collective-permute-start = (f32[16,128]{1,0:T(8,128)S(1)}, f32[16,128]{1,0:T(8,128)S(1)}, u32[]{:S(2)}, u32[]{:S(2)}) collective-permute-start(f32[16,128]{1,0:T(8,128)S(1)} %get-tuple-element.13), channel_id=1, source_target_pairs={{0,64},{32,96},{64,0},{96,32},{1,65},{33,97},{65,1},{97,33},{2,66}... | collective-permute-start | bytes 24584 | tf_op jit(solution)/shard_map/ppermute | solution.py:261
  79.0 5.4 %collective-permute-start.1 = (f32[8,128]{1,0:T(8,128)S(1)}, f32[8,128]{1,0:T(8,128)S(1)}, u32[]{:S(2)}, u32[]{:S(2)}) collective-permute-start(f32[8,128]{1,0:T(8,128)S(1)} %get-tuple-element.15), channel_id=1, source_target_pairs={{0,32},{32,0},{64,96},{96,64},{1,33},{33,1},{65,97},{97,65},{2,34}... | collective-permute-start | bytes 12296 | tf_op jit(solution)/shard_map/ppermute | solution.py:269

commit v5 on v4

--- a/solution.py
+++ b/solution.py
@@ -126,7 +126,7 @@
         multiply(group)
 
 
-def filter_kernel(blocks_ref, out_ref, tall_ref, saved_ref, product_ref):
+def filter_kernel(blocks_ref, out_ref, tall_refs, saved_ref, product_refs):
     parts = blocks_ref.shape[0]
     rows = parts * GROUP
     groups = SIDE
@@ -135,20 +135,25 @@
     col_ids = lax.broadcasted_iota(jnp.int32, (LANES, LANES), 1)
     flip = jnp.where(row_ids + col_ids == LANES - 1, 1.0, 0.0).astype(jnp.bfloat16)
     empty = jnp.zeros((LANES, LANES), jnp.float32)
-    product_ref[:, :LANES] = empty
-    product_ref[:, (parts + 1) * LANES :] = empty
-    tall_ref[rows - GROUP :, LANES:] = jnp.zeros((GROUP, LANES), jnp.bfloat16)
     for group in range(groups):
+        product_refs[group, :, :LANES] = empty
+        product_refs[group, :, (parts + 1) * LANES :] = empty
+        tall_refs[group, rows - GROUP :, LANES:] = jnp.zeros((GROUP, LANES), jnp.bfloat16)
+
+    def multiply(group):
         first = group * GROUP
+        tall_ref, product_ref = tall_refs.at[group], product_refs.at[group]
         for part in range(parts):
             mine = blocks_ref[part, first : first + GROUP, :]
             here = slice(part * GROUP, (part + 1) * GROUP)
             tall_ref[here, :LANES] = mine
             if part > 0:
                 tall_ref[(part - 1) * GROUP : part * GROUP, LANES:] = mine
-            saved_ref[here, :] = blocks_ref[part, channels + first : channels + first + GROUP, :]
+            saved_ref[group, here, :] = blocks_ref[
+                part, channels + first : channels + first + GROUP, :
+            ]
         flipped = lax.dot_general(
-            flip, saved_ref[...], (((1,), (1,)), ((), ())), preferred_element_type=jnp.float32
+            flip, saved_ref[group], (((1,), (1,)), ((), ())), preferred_element_type=jnp.float32
         ).astype(jnp.bfloat16)
         for pair in range(parts // 2):
             start = 2 * pair * GROUP
@@ -156,11 +161,19 @@
             product_ref[:, LANES + pair * SPAN : LANES + (pair + 1) * SPAN] = jnp.dot(
                 flipped[:, :depth], tall_ref[start:, :], preferred_element_type=jnp.float32
             )
-        turned = pltpu.roll(product_ref[...], 1, 1, stride=1, stride_axis=0)
+
+    def add_up(group):
+        turned = pltpu.roll(product_refs[group], 1, 1, stride=1, stride_axis=0)
         line = jnp.sum(turned, axis=0, keepdims=True)
         for part in range(parts):
             start = SPAN + part * LANES
             out_ref[group * parts + part] = line[:, start : start + LANES]
+
+    for group in range(groups):
+        multiply(group)
+        if group > 0:
+            add_up(group - 1)
+    add_up(groups - 1)
 
 
 def split_kernel(came_ref, keep_ref, send_ref, total_ref):
@@ -170,10 +183,10 @@
     for step in range(1, SIDE):
         total = total + came_ref[step * parts : (step + 1) * parts]
     total_ref[...] = total.reshape(parts, LANES)
-    half = lax.axis_index("zh") // 2
+    half = lax.rem(lax.axis_index("zh"), 2)
     for low in range(2):
         here = slice(low * places, (low + 1) * places)
-        mine, other = 2 * half + low, 2 * (1 - half) + low
+        mine, other = 2 * low + half, 2 * low + 1 - half
         keep_ref[here, :] = total_ref[pl.ds(mine, places, stride=SIDE), :]
         send_ref[here, :] = total_ref[pl.ds(other, places, stride=SIDE), :]
 
@@ -181,7 +194,7 @@
 def halve_kernel(kept_ref, came_ref, keep_ref, send_ref, total_ref):
     places = keep_ref.shape[0]
     total_ref[...] = kept_ref[...] + came_ref[...]
-    half = lax.axis_index("zh") % 2
+    half = lax.axis_index("zh") // 2
     keep_ref[...] = total_ref[pl.ds(pl.multiple_of(half * places, places), places), :]
     send_ref[...] = total_ref[pl.ds(pl.multiple_of((1 - half) * places, places), places), :]
 
@@ -233,12 +246,12 @@
         jax.ShapeDtypeStruct((SIDE * parts, 1, LANES), f32),
         blocks,
         scratch=[
-            pltpu.VMEM((2 * half_rows, SPAN), bf16),
-            pltpu.VMEM((2 * half_rows, LANES), bf16),
-            pltpu.VMEM((LANES, length + SPAN), f32),
+            pltpu.VMEM((groups, 2 * half_rows, SPAN), bf16),
+            pltpu.VMEM((groups, 2 * half_rows, LANES), bf16),
+            pltpu.VMEM((groups, LANES, length + SPAN), f32),
         ],
         flops=2**31,
-        vmem=20 * MIB,
+        vmem=24 * MIB,
     )
     lags_came = lax.all_to_all(lags, ("x", "y", "w"), split_axis=0, concat_axis=0, tiled=True)
     input_blocks = call(
@@ -258,22 +271,22 @@
     halves = [jax.ShapeDtypeStruct((2 * places, LANES), f32)] * 2
     whole_places = jax.ShapeDtypeStruct((places, LANES), f32)
     kept, sent = call(split_kernel, halves, lags_came, scratch=[pltpu.VMEM((parts, LANES), f32)])
-    far = lax.ppermute(sent, "zh", [(side, side ^ 2) for side in range(SIDE)])
+    close = lax.ppermute(sent, "zh", [(side, side ^ 1) for side in range(SIDE)])
     kept, sent = call(
         halve_kernel,
         [whole_places] * 2,
         kept,
-        far,
+        close,
         scratch=[pltpu.VMEM((2 * places, LANES), f32)],
     )
-    near = lax.ppermute(sent, "zh", [(side, side ^ 1) for side in range(SIDE)])
+    distant = lax.ppermute(sent, "zh", [(side, side ^ 2) for side in range(SIDE)])
     scale = 1.0 / math.sqrt(GROUP * seqs * length)
     input_grad, filter_part = call(
         lambda *refs: last_kernel(scale, *refs),
         [jax.ShapeDtypeStruct((tokens, width), bf16), whole_places],
         returned,
         kept,
-        near,
+        distant,
         vmem=4 * MIB,
     )
     return (input_grad[None], filter_part.T)

time: 86.7 us -> 86.8 us (level)
  no operation moved by 1% of the time
where the time goes in v5:
time: 86.8 us; the launch traced here: 86.3 us
  blocking collectives  40.7 us (47%)
  starting transfers between devices  25.3 us (29%)
  waiting for transfers between devices  10.2 us (12%)
  Pallas kernels  9.36 us (11%)
    all_to_all x1, blocking collectives, on_device(): lax.all_to_all(packed, ('y', 'w'), split_axis=0, concat_axis=0, tiled=True)  40.7 us
    pallas_call x6, Pallas kernels, call(): pl.pallas_call(kernel, out_shape=out_shape, in_specs=[given] * len(operan...  9.36 us
    ppermute x1, starting transfers between devices, on_device(): lax.ppermute(sent, 'zh', [(side, side ^ 2) for side in range(SIDE)])  8.18 us
    all_to_all x1, waiting for transfers between devices, on_device(): lax.all_to_all(lags, ('x', 'y', 'w'), split_axis=0, concat_axis=0, tiled=...  7.19 us
    all_to_all x1, starting transfers between devices, on_device(): lax.all_to_all(lags, ('x', 'y', 'w'), split_axis=0, concat_axis=0, tiled=...  7.12 us
    ppermute x1, starting transfers between devices, on_device(): close = lax.ppermute(sent, 'zh', [(side, side ^ 1) for side in range(SIDE)])  5.81 us
    all_to_all x1, starting transfers between devices, on_device(): lax.all_to_all(input_blocks, ('y', 'w'), split_axis=0, concat_axis=0, til...  4.18 us
  transfers between devices with their start and end apart: 4, of which 4 were waited for; matrix products, arithmetic and copies ran while one was open for 0% of the time, Pallas kernels for 4%

profile of v5, /device:TPU:1, one launch (start us, length us, event | category | flops | bytes accessed | tf_op | source)
XLA Modules:
  0.0 86.3 jit_solution(2471636440954763322)
XLA Ops:
  0.6 1.6 %shard_map.50 = bf16[8,4,136,128]{3,2,1,0:T(8,128)(2,1)S(1)} custom-call(bf16[128,2048]{1,0:T(8,128)(2,1)} %bitcast.6, bf16[128,2048]{1,0:T(8,128)(2,1)} %bitcast.7, bf16[128,128]{1,0:T(8,128)(2,1)} %filt_hbm.1), custom_call_target="tpu_custom_call" | custom-call | flops 1048576 | bytes 1048576 | tf_op jit(solution)/shard_map/pallas_call | solution.py:21
  2.2 40.7 %all_to_all.15.blocks_ref = bf16[32,136,128]{2,1,0:T(8,128)(2,1)S(1)} all-to-all(bf16[32,136,128]{2,1,0:T(8,128)(2,1)S(1)} %bitcast.5), channel_id=1, replica_groups=mesh['x'=4,'zh'=4,'y'=8,'w'=4] {'y','w'}, dimensions={0} | all-to-all | bytes 2228224 | tf_op jit(solution)/shard_map/all_to_all | solution.py:243
  42.9 3.4 %shard_map.52 = f32[128,1,128]{2,1,0:T(1,128)} custom-call(bf16[32,136,128]{2,1,0:T(8,128)(2,1)S(1)} %all_to_all.15.blocks_ref), custom_call_target="tpu_custom_call" | custom-call | flops 2147483648 | bytes 1048576 | tf_op jit(solution)/shard_map/pallas_call | solution.py:21
  46.3 7.1 %all-to-all-start.1 = ((f32[128,1,128]{2,1,0:T(1,128)}), f32[128,1,128]{2,1,0:T(1,128)S(1)}, u32[]{:S(2)}, u32[]{:S(2)}) async-start(f32[128,1,128]{2,1,0:T(1,128)} %shard_map.52), calls=%async_computation.1 | async-start | bytes 131072 | tf_op jit(solution)/shard_map/all_to_all | solution.py:256
  53.4 3.4 %shard_map.51 = bf16[32,64,128]{2,1,0:T(8,128)(2,1)} custom-call(bf16[32,136,128]{2,1,0:T(8,128)(2,1)S(1)} %all_to_all.15.blocks_ref), custom_call_target="tpu_custom_call" | custom-call | flops 2147483648 | bytes 1048576 | tf_op jit(solution)/shard_map/pallas_call | solution.py:21
  56.8 7.2 %all-to-all-done.1.came_ref = f32[128,1,128]{2,1,0:T(1,128)S(1)} async-done(((f32[128,1,128]{2,1,0:T(1,128)}), f32[128,1,128]{2,1,0:T(1,128)S(1)}, u32[]{:S(2)}, u32[]{:S(2)}) %all-to-all-start.1) | async-done | bytes 65568 | tf_op jit(solution)/shard_map/all_to_all | solution.py:256
  64.0 4.2 %all-to-all-start.2 = ((bf16[32,64,128]{2,1,0:T(8,128)(2,1)}), bf16[32,64,128]{2,1,0:T(8,128)(2,1)S(1)}, u32[]{:S(2)}, u32[]{:S(2)}) async-start(bf16[32,64,128]{2,1,0:T(8,128)(2,1)} %shard_map.51), calls=%async_computation.2 | async-start | bytes 1048576 | tf_op jit(solution)/shard_map/all_to_all | solution.py:270
  68.2 5.8 %collective-permute-start = (f32[16,128]{1,0:T(8,128)S(1)}, f32[16,128]{1,0:T(8,128)S(1)}, u32[]{:S(2)}, u32[]{:S(2)}) collective-permute-start(f32[16,128]{1,0:T(8,128)S(1)} %get-tuple-element.13), channel_id=1, source_target_pairs={{0,32},{32,0},{64,96},{96,64},{1,33},{33,1},{65,97},{97,65},{2,34}... | collective-permute-start | bytes 24584 | tf_op jit(solution)/shard_map/ppermute | solution.py:274
  74.0 1.3 %collective-permute-done.came_ref = f32[16,128]{1,0:T(8,128)S(1)} collective-permute-done((f32[16,128]{1,0:T(8,128)S(1)}, f32[16,128]{1,0:T(8,128)S(1)}, u32[]{:S(2)}, u32[]{:S(2)}) %collective-permute-start) | collective-permute-done | bytes 8224 | tf_op jit(solution)/shard_map/ppermute | solution.py:274
  75.4 8.2 %collective-permute-start.1 = (f32[8,128]{1,0:T(8,128)S(1)}, f32[8,128]{1,0:T(8,128)S(1)}, u32[]{:S(2)}, u32[]{:S(2)}) collective-permute-start(f32[8,128]{1,0:T(8,128)S(1)} %get-tuple-element.15), channel_id=1, source_target_pairs={{0,64},{32,96},{64,0},{96,32},{1,65},{33,97},{65,1},{97,33},{2,66}... | collective-permute-start | bytes 12296 | tf_op jit(solution)/shard_map/ppermute | solution.py:282
  83.6 1.0 %collective-permute-done.1.refs_2_ = f32[8,128]{1,0:T(8,128)S(1)} collective-permute-done((f32[8,128]{1,0:T(8,128)S(1)}, f32[8,128]{1,0:T(8,128)S(1)}, u32[]{:S(2)}, u32[]{:S(2)}) %collective-permute-start.1) | collective-permute-done | bytes 4128 | tf_op jit(solution)/shard_map/ppermute | solution.py:282
  84.6 0.7 all-to-all-done.2.refs_0_
  85.3 1.0 %shard_map.55 = (bf16[128,2048]{1,0:T(8,128)(2,1)}, f32[8,128]{1,0:T(8,128)}) custom-call(bf16[32,64,128]{2,1,0:T(8,128)(2,1)S(1)} %all-to-all-done.2.refs_0_, f32[8,128]{1,0:T(8,128)S(1)} %get-tuple-element.14.refs_1_, f32[8,128]{1,0:T(8,128)S(1)} %collective-permute-done.1.refs_2_), custom_call_target="tpu_custom_call" | custom-call | flops 1048576 | bytes 1048576 | tf_op jit(solution)/shard_map/pallas_call | solution.py:21
  (2 shorter events, 0.1 us)
Async XLA Ops:
  46.3 17.7 %all-to-all-start.1 = ((f32[128,1,128]{2,1,0:T(1,128)}), f32[128,1,128]{2,1,0:T(1,128)S(1)}, u32[]{:S(2)}, u32[]{:S(2)}) async-start(f32[128,1,128]{2,1,0:T(1,128)} %shard_map.52), calls=%async_computation.1 | async-start | bytes 131072 | tf_op jit(solution)/shard_map/all_to_all | solution.py:256
  64.0 21.3 %all-to-all-start.2 = ((bf16[32,64,128]{2,1,0:T(8,128)(2,1)}), bf16[32,64,128]{2,1,0:T(8,128)(2,1)S(1)}, u32[]{:S(2)}, u32[]{:S(2)}) async-start(bf16[32,64,128]{2,1,0:T(8,128)(2,1)} %shard_map.51), calls=%async_computation.2 | async-start | bytes 1048576 | tf_op jit(solution)/shard_map/all_to_all | solution.py:270
  68.2 7.1 %collective-permute-start = (f32[16,128]{1,0:T(8,128)S(1)}, f32[16,128]{1,0:T(8,128)S(1)}, u32[]{:S(2)}, u32[]{:S(2)}) collective-permute-start(f32[16,128]{1,0:T(8,128)S(1)} %get-tuple-element.13), channel_id=1, source_target_pairs={{0,32},{32,0},{64,96},{96,64},{1,33},{33,1},{65,97},{97,65},{2,34}... | collective-permute-start | bytes 24584 | tf_op jit(solution)/shard_map/ppermute | solution.py:274
  75.4 9.2 %collective-permute-start.1 = (f32[8,128]{1,0:T(8,128)S(1)}, f32[8,128]{1,0:T(8,128)S(1)}, u32[]{:S(2)}, u32[]{:S(2)}) collective-permute-start(f32[8,128]{1,0:T(8,128)S(1)} %get-tuple-element.15), channel_id=1, source_target_pairs={{0,64},{32,96},{64,0},{96,32},{1,65},{33,97},{65,1},{97,33},{2,66}... | collective-permute-start | bytes 12296 | tf_op jit(solution)/shard_map/ppermute | solution.py:282

commit v6 on v5

--- a/solution.py
+++ b/solution.py
@@ -183,10 +183,10 @@
     for step in range(1, SIDE):
         total = total + came_ref[step * parts : (step + 1) * parts]
     total_ref[...] = total.reshape(parts, LANES)
-    half = lax.rem(lax.axis_index("zh"), 2)
+    half = lax.axis_index("zh") // 2
     for low in range(2):
         here = slice(low * places, (low + 1) * places)
-        mine, other = 2 * low + half, 2 * low + 1 - half
+        mine, other = 2 * half + low, 2 * (1 - half) + low
         keep_ref[here, :] = total_ref[pl.ds(mine, places, stride=SIDE), :]
         send_ref[here, :] = total_ref[pl.ds(other, places, stride=SIDE), :]
 
@@ -194,7 +194,7 @@
 def halve_kernel(kept_ref, came_ref, keep_ref, send_ref, total_ref):
     places = keep_ref.shape[0]
     total_ref[...] = kept_ref[...] + came_ref[...]
-    half = lax.axis_index("zh") // 2
+    half = lax.axis_index("zh") % 2
     keep_ref[...] = total_ref[pl.ds(pl.multiple_of(half * places, places), places), :]
     send_ref[...] = total_ref[pl.ds(pl.multiple_of((1 - half) * places, places), places), :]
 
@@ -271,22 +271,22 @@
     halves = [jax.ShapeDtypeStruct((2 * places, LANES), f32)] * 2
     whole_places = jax.ShapeDtypeStruct((places, LANES), f32)
     kept, sent = call(split_kernel, halves, lags_came, scratch=[pltpu.VMEM((parts, LANES), f32)])
-    close = lax.ppermute(sent, "zh", [(side, side ^ 1) for side in range(SIDE)])
+    far = lax.ppermute(sent, "zh", [(side, side ^ 2) for side in range(SIDE)])
     kept, sent = call(
         halve_kernel,
         [whole_places] * 2,
         kept,
-        close,
+        far,
         scratch=[pltpu.VMEM((2 * places, LANES), f32)],
     )
-    distant = lax.ppermute(sent, "zh", [(side, side ^ 2) for side in range(SIDE)])
+    near = lax.ppermute(sent, "zh", [(side, side ^ 1) for side in range(SIDE)])
     scale = 1.0 / math.sqrt(GROUP * seqs * length)
     input_grad, filter_part = call(
         lambda *refs: last_kernel(scale, *refs),
         [jax.ShapeDtypeStruct((tokens, width), bf16), whole_places],
         returned,
         kept,
-        distant,
+        near,
         vmem=4 * MIB,
     )
     return (input_grad[None], filter_part.T)

time: 86.8 us -> 86.7 us (level)
  no operation moved by 1% of the time
where the time goes in v6:
time: 86.7 us; the launch traced here: 86.3 us
  blocking collectives  40.7 us (47%)
  starting transfers between devices  25.1 us (29%)
  waiting for transfers between devices  10.4 us (12%)
  Pallas kernels  9.36 us (11%)
    all_to_all x1, blocking collectives, on_device(): lax.all_to_all(packed, ('y', 'w'), split_axis=0, concat_axis=0, tiled=True)  40.7 us
    ppermute x1, starting transfers between devices, on_device(): far = lax.ppermute(sent, 'zh', [(side, side ^ 2) for side in range(SIDE)])  9.74 us
    pallas_call x6, Pallas kernels, call(): pl.pallas_call(kernel, out_shape=out_shape, in_specs=[given] * len(operan...  9.36 us
    all_to_all x1, waiting for transfers between devices, on_device(): lax.all_to_all(lags, ('x', 'y', 'w'), split_axis=0, concat_axis=0, tiled=...  7.19 us
    all_to_all x1, starting transfers between devices, on_device(): lax.all_to_all(lags, ('x', 'y', 'w'), split_axis=0, concat_axis=0, tiled=...  7.12 us
    all_to_all x1, starting transfers between devices, on_device(): lax.all_to_all(input_blocks, ('y', 'w'), split_axis=0, concat_axis=0, til...  4.18 us
    ppermute x1, starting transfers between devices, on_device(): near = lax.ppermute(sent, 'zh', [(side, side ^ 1) for side in range(SIDE)])  4.09 us
  transfers between devices with their start and end apart: 4, of which 4 were waited for; matrix products, arithmetic and copies ran while one was open for 0% of the time, Pallas kernels for 4%

profile of v6, /device:TPU:1, one launch (start us, length us, event | category | flops | bytes accessed | tf_op | source)
XLA Modules:
  0.0 86.3 jit_solution(1523114747437708150)
XLA Ops:
  0.6 1.6 %shard_map.50 = bf16[8,4,136,128]{3,2,1,0:T(8,128)(2,1)S(1)} custom-call(bf16[128,2048]{1,0:T(8,128)(2,1)} %bitcast.6, bf16[128,2048]{1,0:T(8,128)(2,1)} %bitcast.7, bf16[128,128]{1,0:T(8,128)(2,1)} %filt_hbm.1), custom_call_target="tpu_custom_call" | custom-call | flops 1048576 | bytes 1048576 | tf_op jit(solution)/shard_map/pallas_call | solution.py:21
  2.2 40.7 %all_to_all.15.blocks_ref = bf16[32,136,128]{2,1,0:T(8,128)(2,1)S(1)} all-to-all(bf16[32,136,128]{2,1,0:T(8,128)(2,1)S(1)} %bitcast.5), channel_id=1, replica_groups=mesh['x'=4,'zh'=4,'y'=8,'w'=4] {'y','w'}, dimensions={0} | all-to-all | bytes 2228224 | tf_op jit(solution)/shard_map/all_to_all | solution.py:243
  42.9 3.4 %shard_map.52 = f32[128,1,128]{2,1,0:T(1,128)} custom-call(bf16[32,136,128]{2,1,0:T(8,128)(2,1)S(1)} %all_to_all.15.blocks_ref), custom_call_target="tpu_custom_call" | custom-call | flops 2147483648 | bytes 1048576 | tf_op jit(solution)/shard_map/pallas_call | solution.py:21
  46.3 7.1 %all-to-all-start.1 = ((f32[128,1,128]{2,1,0:T(1,128)}), f32[128,1,128]{2,1,0:T(1,128)S(1)}, u32[]{:S(2)}, u32[]{:S(2)}) async-start(f32[128,1,128]{2,1,0:T(1,128)} %shard_map.52), calls=%async_computation.1 | async-start | bytes 131072 | tf_op jit(solution)/shard_map/all_to_all | solution.py:256
  53.4 3.4 %shard_map.51 = bf16[32,64,128]{2,1,0:T(8,128)(2,1)} custom-call(bf16[32,136,128]{2,1,0:T(8,128)(2,1)S(1)} %all_to_all.15.blocks_ref), custom_call_target="tpu_custom_call" | custom-call | flops 2147483648 | bytes 1048576 | tf_op jit(solution)/shard_map/pallas_call | solution.py:21
  56.8 7.2 %all-to-all-done.1.came_ref = f32[128,1,128]{2,1,0:T(1,128)S(1)} async-done(((f32[128,1,128]{2,1,0:T(1,128)}), f32[128,1,128]{2,1,0:T(1,128)S(1)}, u32[]{:S(2)}, u32[]{:S(2)}) %all-to-all-start.1) | async-done | bytes 65568 | tf_op jit(solution)/shard_map/all_to_all | solution.py:256
  64.0 4.2 %all-to-all-start.2 = ((bf16[32,64,128]{2,1,0:T(8,128)(2,1)}), bf16[32,64,128]{2,1,0:T(8,128)(2,1)S(1)}, u32[]{:S(2)}, u32[]{:S(2)}) async-start(bf16[32,64,128]{2,1,0:T(8,128)(2,1)} %shard_map.51), calls=%async_computation.2 | async-start | bytes 1048576 | tf_op jit(solution)/shard_map/all_to_all | solution.py:270
  68.2 9.7 %collective-permute-start = (f32[16,128]{1,0:T(8,128)S(1)}, f32[16,128]{1,0:T(8,128)S(1)}, u32[]{:S(2)}, u32[]{:S(2)}) collective-permute-start(f32[16,128]{1,0:T(8,128)S(1)} %get-tuple-element.13), channel_id=1, source_target_pairs={{0,64},{32,96},{64,0},{96,32},{1,65},{33,97},{65,1},{97,33},{2,66}... | collective-permute-start | bytes 24584 | tf_op jit(solution)/shard_map/ppermute | solution.py:274
  78.0 1.0 %collective-permute-done.came_ref = f32[16,128]{1,0:T(8,128)S(1)} collective-permute-done((f32[16,128]{1,0:T(8,128)S(1)}, f32[16,128]{1,0:T(8,128)S(1)}, u32[]{:S(2)}, u32[]{:S(2)}) %collective-permute-start) | collective-permute-done | bytes 8224 | tf_op jit(solution)/shard_map/ppermute | solution.py:274
  79.0 4.1 %collective-permute-start.1 = (f32[8,128]{1,0:T(8,128)S(1)}, f32[8,128]{1,0:T(8,128)S(1)}, u32[]{:S(2)}, u32[]{:S(2)}) collective-permute-start(f32[8,128]{1,0:T(8,128)S(1)} %get-tuple-element.15), channel_id=1, source_target_pairs={{0,32},{32,0},{64,96},{96,64},{1,33},{33,1},{65,97},{97,65},{2,34}... | collective-permute-start | bytes 12296 | tf_op jit(solution)/shard_map/ppermute | solution.py:282
  83.1 1.3 %collective-permute-done.1.refs_2_ = f32[8,128]{1,0:T(8,128)S(1)} collective-permute-done((f32[8,128]{1,0:T(8,128)S(1)}, f32[8,128]{1,0:T(8,128)S(1)}, u32[]{:S(2)}, u32[]{:S(2)}) %collective-permute-start.1) | collective-permute-done | bytes 4128 | tf_op jit(solution)/shard_map/ppermute | solution.py:282
  84.4 0.8 all-to-all-done.2.refs_0_
  85.3 1.0 %shard_map.55 = (bf16[128,2048]{1,0:T(8,128)(2,1)}, f32[8,128]{1,0:T(8,128)}) custom-call(bf16[32,64,128]{2,1,0:T(8,128)(2,1)S(1)} %all-to-all-done.2.refs_0_, f32[8,128]{1,0:T(8,128)S(1)} %get-tuple-element.14.refs_1_, f32[8,128]{1,0:T(8,128)S(1)} %collective-permute-done.1.refs_2_), custom_call_target="tpu_custom_call" | custom-call | flops 1048576 | bytes 1048576 | tf_op jit(solution)/shard_map/pallas_call | solution.py:21
  (2 shorter events, 0.1 us)
Async XLA Ops:
  46.3 17.7 %all-to-all-start.1 = ((f32[128,1,128]{2,1,0:T(1,128)}), f32[128,1,128]{2,1,0:T(1,128)S(1)}, u32[]{:S(2)}, u32[]{:S(2)}) async-start(f32[128,1,128]{2,1,0:T(1,128)} %shard_map.52), calls=%async_computation.1 | async-start | bytes 131072 | tf_op jit(solution)/shard_map/all_to_all | solution.py:256
  64.0 21.3 %all-to-all-start.2 = ((bf16[32,64,128]{2,1,0:T(8,128)(2,1)}), bf16[32,64,128]{2,1,0:T(8,128)(2,1)S(1)}, u32[]{:S(2)}, u32[]{:S(2)}) async-start(bf16[32,64,128]{2,1,0:T(8,128)(2,1)} %shard_map.51), calls=%async_computation.2 | async-start | bytes 1048576 | tf_op jit(solution)/shard_map/all_to_all | solution.py:270
  68.2 10.8 %collective-permute-start = (f32[16,128]{1,0:T(8,128)S(1)}, f32[16,128]{1,0:T(8,128)S(1)}, u32[]{:S(2)}, u32[]{:S(2)}) collective-permute-start(f32[16,128]{1,0:T(8,128)S(1)} %get-tuple-element.13), channel_id=1, source_target_pairs={{0,64},{32,96},{64,0},{96,32},{1,65},{33,97},{65,1},{97,33},{2,66}... | collective-permute-start | bytes 24584 | tf_op jit(solution)/shard_map/ppermute | solution.py:274
  79.0 5.4 %collective-permute-start.1 = (f32[8,128]{1,0:T(8,128)S(1)}, f32[8,128]{1,0:T(8,128)S(1)}, u32[]{:S(2)}, u32[]{:S(2)}) collective-permute-start(f32[8,128]{1,0:T(8,128)S(1)} %get-tuple-element.15), channel_id=1, source_target_pairs={{0,32},{32,0},{64,96},{96,64},{1,33},{33,1},{65,97},{97,65},{2,34}... | collective-permute-start | bytes 12296 | tf_op jit(solution)/shard_map/ppermute | solution.py:282
